TPU v7x, 32 devices: a whole 2x2x4 slice. The times are simulated.
32 devices in a mesh: fsdp: 16 (over z, y, x), seq: 2 (over core).
Axes of the slice: x: 2, y: 2, z: 4, core: 2. Of those that a mesh axis runs over, the one named last changes fastest.
Arguments:
- layer_input: bfloat16 [64, 1024, 576], P('fsdp', 'seq'), may hold values from -6 to 6
- segments: int32 [64, 1024], P('fsdp'), may hold values from 0 to 6, as said below
- project_weight: bfloat16 [552960], P(('fsdp', 'seq')), may hold values from -0.25 to 0.25
- output_weight: bfloat16 [331776], P(('fsdp', 'seq')), may hold values from -1 to 1
- gate_up_weight: bfloat16 [1769472], P(('fsdp', 'seq')), may hold values from -0.25 to 0.25
- down_weight: bfloat16 [884736], P(('fsdp', 'seq')), may hold values from -0.15625 to 0.15625
- gains: bfloat16 [1152], P('fsdp'), may hold values from 0.5 to 1.5
- cotangent: bfloat16 [64, 1024, 576], P('fsdp', 'seq'), may hold values from -6 to 6
Outputs:
- result: bfloat16 [64, 1024, 576], P('fsdp', 'seq')
- input_gradient: bfloat16 [64, 1024, 576], P('fsdp', 'seq')
- project_gradient: float32 [552960], P(('fsdp', 'seq'))
- output_gradient: float32 [331776], P(('fsdp', 'seq'))
- gate_up_gradient: float32 [1769472], P(('fsdp', 'seq'))
- down_gradient: float32 [884736], P(('fsdp', 'seq'))
- gains_gradient: float32 [1152], P('fsdp')
Inputs may be any that keep to these rules, and one draw needn't show every extreme that they name: `segments`: in each sequence the segment numbers never fall, start at 0 and take each of the seven values 0 to 6; document 3 covers positions 256 through 3 * 256.
All inputs are finite; a program needn't handle non-finite values.
Results may differ from a plain program's by a relative error of at most 0.012.
Values may be sent and summed in bfloat16 or wider, within the bound.
A program may use at most 192 MiB of HBM per device.

v0:
```python
import jax
import jax.numpy as jnp
from jax import lax
from jax.sharding import PartitionSpec as P

D = 576
H = 9
KV = 3
HD = 64
FF = 1536


EPSILON = 1e-05
THETA = 100000.0
MASKED = -1e30


def shifted(block, axis, distance):
    devices = range(lax.axis_size(axis))
    route = [(i - distance, i) for i in devices if i - distance in devices]
    return lax.ppermute(block, axis, route)


def root_norm(values, gain):
    return values * lax.rsqrt(jnp.mean(values * values, axis=-1, keepdims=True) + EPSILON) * gain


def rotary_tables(positions, size):
    rates = THETA ** (-(jnp.arange(size // 2, dtype=jnp.float32) * 2.0) / size)
    angle = positions.astype(jnp.float32)[:, None] * rates[None, :]
    return (jnp.cos(angle), jnp.sin(angle))


def rotate(values, cosine, sine):
    middle = values.shape[-1] // 2
    first = values[..., :middle]
    second = values[..., middle:]
    cosine_row = cosine[:, None, :]
    sine_row = sine[:, None, :]
    return jnp.concatenate(
        [first * cosine_row - second * sine_row, second * cosine_row + first * sine_row], axis=-1
    )


def gated_unit(gate_up_activations):
    middle = gate_up_activations.shape[-1] // 2
    return jax.nn.silu(gate_up_activations[..., :middle]) * gate_up_activations[..., middle:]


def shape_weights(gathered):
    return (
        gathered[0].reshape(D, (H + 2 * KV) * HD),
        gathered[1].reshape(H * HD, D),
        gathered[2].reshape(D, 2 * FF),
        gathered[3].reshape(FF, D),
    )


def per_device(
    layer_input,
    segments,
    project_weight,
    output_weight,
    gate_up_weight,
    down_weight,
    gains,
    cotangent,
):
    sequences = layer_input.shape[0]
    half = layer_input.shape[1]
    groups = H // KV
    scale = HD ** (-0.5)
    gathered = (
        lax.all_gather(project_weight, ("fsdp", "seq"), axis=0, tiled=True),
        lax.all_gather(output_weight, ("fsdp", "seq"), axis=0, tiled=True),
        lax.all_gather(gate_up_weight, ("fsdp", "seq"), axis=0, tiled=True),
        lax.all_gather(down_weight, ("fsdp", "seq"), axis=0, tiled=True),
    )
    gain_whole = lax.all_gather(gains, "fsdp", axis=0, tiled=True)
    attention_project_matrix, output_projection_matrix, gate_up_matrix, down_projection_matrix = (
        shape_weights(gathered)
    )
    start = lax.axis_index("seq") * half
    positions = start + jnp.arange(half, dtype=jnp.int32)
    key_places = start - half + jnp.arange(2 * half, dtype=jnp.int32)
    query_labels = lax.dynamic_slice_in_dim(segments, start, half, axis=1)
    padded = jnp.concatenate([jnp.full((sequences, half), -1, jnp.int32), segments], axis=1)
    key_labels = lax.dynamic_slice_in_dim(padded, start, 2 * half, axis=1)
    cosine, sine = rotary_tables(positions, HD)
    hidden_features = layer_input.astype(jnp.float32)
    normalized_input_bfloat = root_norm(hidden_features, gain_whole[:D].astype(jnp.float32)).astype(
        jnp.bfloat16
    )
    projected_rows = jnp.einsum(
        "fwq,qa->fwa",
        normalized_input_bfloat,
        attention_project_matrix,
        preferred_element_type=jnp.float32,
    )
    width_rotated = (H + KV) * HD

    def rotary_part(columns):
        queries = rotate(columns[..., : H * HD].reshape(sequences, half, H, HD), cosine, sine)
        keys = rotate(columns[..., H * HD :].reshape(sequences, half, KV, HD), cosine, sine)
        return (queries, keys)

    (queries, keys), rotary_pull = jax.vjp(rotary_part, projected_rows[..., :width_rotated])
    queries_low = queries.astype(jnp.bfloat16)
    keys_low = keys.astype(jnp.bfloat16)
    values_low = (
        projected_rows[..., width_rotated:].reshape(sequences, half, KV, HD).astype(jnp.bfloat16)
    )
    remote_keys, remote_values = shifted((keys_low, values_low), "seq", 1)
    keys_all = jnp.concatenate([remote_keys, keys_low], axis=1)
    values_all = jnp.concatenate([remote_values, values_low], axis=1)

    def allowed_of(query_row, key_row):
        return (key_places[None, :] <= positions[:, None]) & (
            key_row[None, :] == query_row[:, None]
        )

    def scores_of(query, key):
        grouped = query.reshape(half, KV, groups, HD)
        return (
            grouped,
            jnp.einsum("tkgd,skd->kgts", grouped, key, preferred_element_type=jnp.float32) * scale,
        )

    def forward_one(item):
        query, key, value, query_row, key_row = item
        grouped, scores = scores_of(query, key)
        scores = jnp.where(allowed_of(query_row, key_row), scores, MASKED)
        top = jnp.max(scores, axis=-1, keepdims=True)
        powers = jnp.exp(scores - top)
        total = jnp.sum(powers, axis=-1, keepdims=True)
        weights = (powers / total).astype(jnp.bfloat16)
        attention_mixed = jnp.einsum(
            "kgts,skd->tkgd", weights, value, preferred_element_type=jnp.float32
        )
        return (attention_mixed.reshape(half, H * HD), top + jnp.log(total))

    attention_mixed, log_total = lax.map(
        forward_one, (queries_low, keys_all, values_all, query_labels, key_labels)
    )
    attention_mixed_bfloat = attention_mixed.astype(jnp.bfloat16)
    residual_stream = hidden_features + jnp.einsum(
        "crz,zm->crm",
        attention_mixed_bfloat,
        output_projection_matrix,
        preferred_element_type=jnp.float32,
    )
    mixer_output_bfloat = root_norm(residual_stream, gain_whole[D:].astype(jnp.float32)).astype(
        jnp.bfloat16
    )
    gate_up_activations = jnp.einsum(
        "mar,rw->maw", mixer_output_bfloat, gate_up_matrix, preferred_element_type=jnp.float32
    )
    hidden_state, unit_pull = jax.vjp(gated_unit, gate_up_activations)
    hidden_state_bfloat = hidden_state.astype(jnp.bfloat16)
    result = (
        residual_stream
        + jnp.einsum(
            "gvc,cr->gvr",
            hidden_state_bfloat,
            down_projection_matrix,
            preferred_element_type=jnp.float32,
        )
    ).astype(jnp.bfloat16)
    gathered = (
        lax.all_gather(project_weight, ("fsdp", "seq"), axis=0, tiled=True),
        lax.all_gather(output_weight, ("fsdp", "seq"), axis=0, tiled=True),
        lax.all_gather(gate_up_weight, ("fsdp", "seq"), axis=0, tiled=True),
        lax.all_gather(down_weight, ("fsdp", "seq"), axis=0, tiled=True),
    )
    gain_whole = lax.all_gather(gains, "fsdp", axis=0, tiled=True)
    attention_project_matrix, output_projection_matrix, gate_up_matrix, down_projection_matrix = (
        shape_weights(gathered)
    )
    delta_down = jnp.einsum(
        "rqh,rqo->ho", hidden_state_bfloat, cotangent, preferred_element_type=jnp.float32
    )
    delta_hidden = jnp.einsum(
        "iou,eu->ioe", cotangent, down_projection_matrix, preferred_element_type=jnp.float32
    )
    gate_up_cotangent = unit_pull(delta_hidden)[0].astype(jnp.bfloat16)
    delta_gate_up_mat = jnp.einsum(
        "bqg,bqv->gv", mixer_output_bfloat, gate_up_cotangent, preferred_element_type=jnp.float32
    )
    delta_mixer = jnp.einsum(
        "evi,ai->eva", gate_up_cotangent, gate_up_matrix, preferred_element_type=jnp.float32
    )
    mixer_pull = jax.vjp(root_norm, residual_stream, gain_whole[D:].astype(jnp.float32))[1]
    delta_residual, delta_gain_mixer = mixer_pull(delta_mixer)
    delta_residual = delta_residual + cotangent.astype(jnp.float32)
    branch_gradient = delta_residual.astype(jnp.bfloat16)
    delta_output_mat = jnp.einsum(
        "zxa,zxq->aq", attention_mixed_bfloat, branch_gradient, preferred_element_type=jnp.float32
    )
    delta_mixed = jnp.einsum(
        "wrc,jc->wrj", branch_gradient, output_projection_matrix, preferred_element_type=jnp.float32
    ).astype(jnp.bfloat16)

    def backward_one(item):
        query, key, value, query_row, key_row, log_row, delta_row = item
        grouped, scores = scores_of(query, key)
        probs = jnp.where(allowed_of(query_row, key_row), jnp.exp(scores - log_row), 0.0)
        delta_grouped = delta_row.reshape(half, KV, groups, HD)
        delta_probs = jnp.einsum(
            "tkgd,skd->kgts", delta_grouped, value, preferred_element_type=jnp.float32
        )
        row_dot = jnp.sum(probs * delta_probs, axis=-1, keepdims=True)
        delta_scores = (probs * (delta_probs - row_dot)).astype(jnp.bfloat16)
        delta_query = (
            jnp.einsum("kgts,skd->tkgd", delta_scores, key, preferred_element_type=jnp.float32)
            * scale
        )
        delta_key = (
            jnp.einsum("kgts,tkgd->skd", delta_scores, grouped, preferred_element_type=jnp.float32)
            * scale
        )
        delta_value = jnp.einsum(
            "kgts,tkgd->skd",
            probs.astype(jnp.bfloat16),
            delta_grouped,
            preferred_element_type=jnp.float32,
        )
        return (delta_query.reshape(half, H, HD), delta_key, delta_value)

    delta_queries, delta_keys, delta_values = lax.map(
        backward_one,
        (queries_low, keys_all, values_all, query_labels, key_labels, log_total, delta_mixed),
    )
    back_keys, back_values = (
        shifted(delta_keys[:, :half].astype(jnp.bfloat16), "seq", -1).astype(jnp.float32),
        shifted(delta_values[:, :half].astype(jnp.bfloat16), "seq", -1).astype(jnp.float32),
    )
    delta_keys = delta_keys[:, half:] + back_keys
    delta_values = delta_values[:, half:] + back_values
    delta_rotated = rotary_pull((delta_queries, delta_keys))[0]
    projected_cotangent = jnp.concatenate(
        [delta_rotated, delta_values.reshape(sequences, half, KV * HD)], axis=-1
    ).astype(jnp.bfloat16)
    delta_project_mat = jnp.einsum(
        "zgv,zgf->vf",
        normalized_input_bfloat,
        projected_cotangent,
        preferred_element_type=jnp.float32,
    )
    delta_normed = jnp.einsum(
        "xgc,fc->xgf",
        projected_cotangent,
        attention_project_matrix,
        preferred_element_type=jnp.float32,
    )
    attend_pull = jax.vjp(root_norm, hidden_features, gain_whole[:D].astype(jnp.float32))[1]
    delta_features, delta_gain_attend = attend_pull(delta_normed)
    input_gradient = (delta_residual + delta_features).astype(jnp.bfloat16)
    project_gradient, output_gradient, gate_up_gradient, down_gradient = (
        lax.psum_scatter(
            delta_project_mat.reshape(-1), ("fsdp", "seq"), scatter_dimension=0, tiled=True
        ),
        lax.psum_scatter(
            delta_output_mat.reshape(-1), ("fsdp", "seq"), scatter_dimension=0, tiled=True
        ),
        lax.psum_scatter(
            delta_gate_up_mat.reshape(-1), ("fsdp", "seq"), scatter_dimension=0, tiled=True
        ),
        lax.psum_scatter(delta_down.reshape(-1), ("fsdp", "seq"), scatter_dimension=0, tiled=True),
    )
    gain_total = lax.psum(jnp.concatenate([delta_gain_attend, delta_gain_mixer]), "seq")
    gains_gradient = lax.psum_scatter(gain_total, "fsdp", scatter_dimension=0, tiled=True)
    return (
        result,
        input_gradient,
        project_gradient,
        output_gradient,
        gate_up_gradient,
        down_gradient,
        gains_gradient,
    )


def solution(mesh):
    return jax.shard_map(
        per_device,
        mesh=mesh,
        in_specs=(
            P("fsdp", "seq", None),
            P("fsdp", None),
            P(("fsdp", "seq")),
            P(("fsdp", "seq")),
            P(("fsdp", "seq")),
            P(("fsdp", "seq")),
            P("fsdp"),
            P("fsdp", "seq", None),
        ),
        out_specs=(
            P("fsdp", "seq", None),
            P("fsdp", "seq", None),
            P(("fsdp", "seq")),
            P(("fsdp", "seq")),
            P(("fsdp", "seq")),
            P(("fsdp", "seq")),
            P("fsdp"),
        ),
        check_vma=False,
    )
```

profile of v0, /device:TPU:0, one launch (start us, length us, event | category | flops | bytes accessed | tf_op | source)
XLA Modules:
  0.0 912.1 jit_solution(465461058786496717)
XLA Ops:
  13.2 43.6 %all-reduce.9 = bf16[1152]{0:T(1024)(128)(2,1)S(1)} all-reduce(bf16[1152]{0:T(1024)(128)(2,1)S(1)} %dynamic-update-slice), channel_id=1, replica_groups=mesh['fsdp'=16,'seq'=2] {'fsdp'}, use_global_device_ids=true, to_apply=%add.9 | all-reduce | flops 1152 | bytes 4608
  61.1 43.7 %all-gather.1 = bf16[32,1,10368]{2,1,0:T(2,128)(2,1)} all-gather(bf16[1,1,10368]{2,1,0:T(2,128)(2,1)S(1)} %reshape.231), channel_id=1, replica_groups=mesh['fsdp'=16,'seq'=2] {'fsdp','seq'}, dimensions={0}, use_global_device_ids=true | all-gather | bytes 684288 | tf_op jit(solution)/shard_map/all_gather | solution.py:75
  147.8 123.8 %while.28 = (s32[]{:T(128)}, bf16[4,512,576]{1,2,0:T(8,128)(2,1)}, f32[4,3,3,512,1]{3,2,1,4,0:T(4,128)}, bf16[4,1024,3,64]{1,3,2,0:T(8,128)(2,1)}, s32[4,1024]{1...) while((s32[]{:T(128)}, bf16[4,512,576]{1,2,0:T(8,128)(2,1)}, ...), condition=%wide.region_4.5_spmd.clone, body=%wide.region_1.4_spmd.clone.sunk | while | flops 1266152448 | bytes 63230104 | solution.py:142
  158.1 10.2 %fusion.127 = f32[3,3,512]{2,1,0:T(4,128)S(1)} fusion(f32[3,1024,512,3]{2,1,3,0:T(8,128)} %get-tuple-element.400, f32[3,3,512]{2,1,0:T(4,128)S(1)} %get-tuple-element.401, pred[512,1024]{0,1:T(8,128)(4,1)S(1)} %compare_and_fusion.4), kind=kLoop, calls=%fused_computation.7.clone.1 | loop fusion | flops 18869760 | bytes 19435520 | tf_op jit(solution)/shard_map/while/body/eval_jaxpr/reduce_sum | solution.py:135
  168.4 9.1 fusion.128
  189.1 10.4 %fusion.127 = f32[3,3,512]{2,1,0:T(4,128)S(1)} fusion(f32[3,1024,512,3]{2,1,3,0:T(8,128)} %get-tuple-element.400, f32[3,3,512]{2,1,0:T(4,128)S(1)} %get-tuple-element.401, pred[512,1024]{0,1:T(8,128)(4,1)S(1)} %compare_and_fusion.4), kind=kLoop, calls=%fused_computation.7.clone.1 | loop fusion | flops 18869760 | bytes 19435520 | tf_op jit(solution)/shard_map/while/body/eval_jaxpr/reduce_sum | solution.py:135
  199.5 9.1 fusion.128
  220.1 10.2 %fusion.127 = f32[3,3,512]{2,1,0:T(4,128)S(1)} fusion(f32[3,1024,512,3]{2,1,3,0:T(8,128)} %get-tuple-element.400, f32[3,3,512]{2,1,0:T(4,128)S(1)} %get-tuple-element.401, pred[512,1024]{0,1:T(8,128)(4,1)S(1)} %compare_and_fusion.4), kind=kLoop, calls=%fused_computation.7.clone.1 | loop fusion | flops 18869760 | bytes 19435520 | tf_op jit(solution)/shard_map/while/body/eval_jaxpr/reduce_sum | solution.py:135
  230.3 9.1 fusion.128
  250.8 10.2 %fusion.127 = f32[3,3,512]{2,1,0:T(4,128)S(1)} fusion(f32[3,1024,512,3]{2,1,3,0:T(8,128)} %get-tuple-element.400, f32[3,3,512]{2,1,0:T(4,128)S(1)} %get-tuple-element.401, pred[512,1024]{0,1:T(8,128)(4,1)S(1)} %compare_and_fusion.4), kind=kLoop, calls=%fused_computation.7.clone.1 | loop fusion | flops 18869760 | bytes 19435520 | tf_op jit(solution)/shard_map/while/body/eval_jaxpr/reduce_sum | solution.py:135
  261.0 9.1 fusion.128
  289.9 17.8 %fusion.85 = f32[4,512,3072]{2,1,0:T(8,128)} fusion(bf16[576,3072,1]{1,0,2:T(8,128)(2,1)} %reshape.248, f32[4,512,576]{1,2,0:T(8,128)} %get-tuple-element.266, f32[576]{0:T(1024)} %get-tuple-element.259, f32[4,512]{1,0:T(4,128)} %fusion.80), kind=kOutput, calls=%fused_computation.153 | convolution fusion | flops 7251296256 | bytes 33433856 | tf_op jit(solution)/shard_map/mar,rw->maw/dot_general | solution.py:155
  307.7 23.7 %fusion.70 = (f32[4,512,1536]{2,1,0:T(8,128)}, f32[4,512,1536]{2,1,0:T(8,128)}, bf16[4,512,1536]{2,1,0:T(8,128)(2,1)}) fusion(f32[4,512,3072]{2,1,0:T(8,128)} %fusion.85, bf16[4,512,576]{1,2,0:T(8,128)(2,1)S(1)} %copy-done.8, bf16[1536,576]{1,0:T(8,128)(2,1)S(1)} %reshape.218), kind=kOutput, calls=%fused_computation.122 | convolution fusion | flops 3667918848 | bytes 60751872 | tf_op jit(solution)/shard_map/iou,eu->ioe/dot_general | solution.py:182
  331.4 20.8 %multiply_reduce_fusion = (f32[576]{0:T(1024)}, f32[4,512]{1,0:T(4,128)S(1)}, f32[4,512,576]{1,2,0:T(8,128)}) fusion(f32[4,512,576]{1,2,0:T(8,128)} %get-tuple-element.266, f32[4,512]{1,0:T(4,128)} %fusion.80, f32[576]{0:T(1024)} %get-tuple-element.259, bf16[576,3072,1]{1,0,2:T(8,128)(2,1)} %reshape.248, f32[4,512,1536]{2,1,0:T(8,128)} %get-tuple-element.249, ...), kind=kOutput, calls=%fused_computation.91 | convolution fusion | flops 7267415552 | bytes 38162944 | tf_op jit(solution)/shard_map/evi,ai->eva/dot_general | solution.py:189
  352.2 16.3 %convolution_bitcast_fusion.2 = f32[72,24,8,128]{3,2,1,0:T(8,128)} fusion(f32[4,512,1536]{2,1,0:T(8,128)} %get-tuple-element.249, f32[4,512,1536]{2,1,0:T(8,128)} %get-tuple-element.248, f32[4,512,576]{1,2,0:T(8,128)} %get-tuple-element.266, f32[576]{0:T(1024)S(1)} %copy-done.31, f32[4,512]{1,0:T(4,128)S(1)} %copy-done.26), kind=kOutput, calls=%fused_computation.99 | convolution fusion | flops 7263879168 | bytes 36972800 | tf_op jit(solution)/shard_map/bqg,bqv->gv/dot_general | solution.py:186
  368.5 9.4 %convolution_bitcast_fusion.1 = f32[1536,576]{1,0:T(8,128)} fusion(bf16[4,512,1536]{2,1,0:T(8,128)(2,1)} %get-tuple-element.250, bf16[4,512,576]{1,2,0:T(8,128)(2,1)} %param.19), kind=kOutput, calls=%fused_computation.98 | convolution fusion | flops 3623878656 | bytes 12189696 | tf_op jit(solution)/shard_map/rqh,rqo->ho/dot_general | solution.py:179
  387.4 219.8 %while.29 = (s32[]{:T(128)}, f32[4,512,9,64]{1,3,2,0:T(8,128)}, f32[4,1024,3,64]{1,3,2,0:T(8,128)}, f32[4,1024,3,64]{1,3,2,0:T(8,128)}, bf16[4,1024,3,64]{1,3,2,...) while((s32[]{:T(128)}, f32[4,512,9,64]{1,3,2,0:T(8,128)}, ...), condition=%wide.region_9.10_spmd.clone, body=%wide.region_7.9_spmd.clone.sunk | while | flops 3092739072 | bytes 154824896 | solution.py:229
  400.0 9.2 %fusion.142 = f32[4,1024,3,64]{1,3,2,0:T(8,128)} fusion(f32[4,1024,3,64]{1,3,2,0:T(8,128)} %get-tuple-element.467, s32[]{:T(128)S(6)} %copy.82, bf16[512,3,3,64]{0,3,2,1:T(8,128)(2,1)S(1)} %bitcast.227, f32[3,1024,512,3]{2,1,3,0:T(8,128)} %fusion.138, f32[3,3,512]{2,1,0:T(4,128)S(1)} %dynamic-slice_bitcast_fusion.2, ...), kind=kOutput, calls=%fused_computation.45.clone.1 | convolution fusion | flops 622854144 | bytes 20793348 | tf_op jit(solution)/shard_map/while/body/eval_jaxpr/kgts,tkgd->skd/dot_general | solution.py:221
  409.2 13.1 %fusion.139 = (f32[3,3,512]{2,1,0:T(4,128)S(1)}, f32[3,1024,512,3]{2,1,3,0:T(8,128)}) fusion(f32[3,1024,512,3]{2,1,3,0:T(8,128)} %fusion.138, f32[3,3,512]{2,1,0:T(4,128)S(1)} %dynamic-slice_bitcast_fusion.2, pred[512,1024]{0,1:T(8,128)(4,1)S(1)} %compare_and_fusion.5, bf16[512,3,3,64]{0,3,2,1:T(8,128)(2,1)S(1)} %bitcast.228, ...), kind=kOutput, calls=%fused_computation.29.clone.1 | convolution fusion | flops 627568128 | bytes 39292932 | tf_op jit(solution)/shard_map/while/body/eval_jaxpr/tkgd,skd->kgts/dot_general | solution.py:208
  422.3 13.5 %fusion.140 = bf16[3,3,512,1024]{2,3,1,0:T(8,128)(2,1)S(1)} fusion(f32[3,1024,512,3]{2,1,3,0:T(8,128)} %get-tuple-element.415, f32[3,1024,512,3]{2,1,3,0:T(8,128)} %fusion.138, f32[3,3,512]{2,1,0:T(4,128)S(1)} %get-tuple-element.416, f32[3,3,512]{2,1,0:T(4,128)S(1)} %dynamic-slice_bitcast_fusion.2, pred[512,1024]{0,1:T(8,128)(4,1)S(1)} %compare_and_fusion.5), kind=kLoop, calls=%fused_computation.31.clone.1 | loop fusion | flops 28311552 | bytes 47747072 | tf_op jit(solution)/shard_map/while/body/eval_jaxpr/convert_element_type | solution.py:212
  454.8 9.2 %fusion.142 = f32[4,1024,3,64]{1,3,2,0:T(8,128)} fusion(f32[4,1024,3,64]{1,3,2,0:T(8,128)} %get-tuple-element.467, s32[]{:T(128)S(6)} %copy.82, bf16[512,3,3,64]{0,3,2,1:T(8,128)(2,1)S(1)} %bitcast.227, f32[3,1024,512,3]{2,1,3,0:T(8,128)} %fusion.138, f32[3,3,512]{2,1,0:T(4,128)S(1)} %dynamic-slice_bitcast_fusion.2, ...), kind=kOutput, calls=%fused_computation.45.clone.1 | convolution fusion | flops 622854144 | bytes 20793348 | tf_op jit(solution)/shard_map/while/body/eval_jaxpr/kgts,tkgd->skd/dot_general | solution.py:221
  464.1 13.1 %fusion.139 = (f32[3,3,512]{2,1,0:T(4,128)S(1)}, f32[3,1024,512,3]{2,1,3,0:T(8,128)}) fusion(f32[3,1024,512,3]{2,1,3,0:T(8,128)} %fusion.138, f32[3,3,512]{2,1,0:T(4,128)S(1)} %dynamic-slice_bitcast_fusion.2, pred[512,1024]{0,1:T(8,128)(4,1)S(1)} %compare_and_fusion.5, bf16[512,3,3,64]{0,3,2,1:T(8,128)(2,1)S(1)} %bitcast.228, ...), kind=kOutput, calls=%fused_computation.29.clone.1 | convolution fusion | flops 627568128 | bytes 39292932 | tf_op jit(solution)/shard_map/while/body/eval_jaxpr/tkgd,skd->kgts/dot_general | solution.py:208
  477.1 13.5 %fusion.140 = bf16[3,3,512,1024]{2,3,1,0:T(8,128)(2,1)S(1)} fusion(f32[3,1024,512,3]{2,1,3,0:T(8,128)} %get-tuple-element.415, f32[3,1024,512,3]{2,1,3,0:T(8,128)} %fusion.138, f32[3,3,512]{2,1,0:T(4,128)S(1)} %get-tuple-element.416, f32[3,3,512]{2,1,0:T(4,128)S(1)} %dynamic-slice_bitcast_fusion.2, pred[512,1024]{0,1:T(8,128)(4,1)S(1)} %compare_and_fusion.5), kind=kLoop, calls=%fused_computation.31.clone.1 | loop fusion | flops 28311552 | bytes 47747072 | tf_op jit(solution)/shard_map/while/body/eval_jaxpr/convert_element_type | solution.py:212
  509.7 9.2 %fusion.142 = f32[4,1024,3,64]{1,3,2,0:T(8,128)} fusion(f32[4,1024,3,64]{1,3,2,0:T(8,128)} %get-tuple-element.467, s32[]{:T(128)S(6)} %copy.82, bf16[512,3,3,64]{0,3,2,1:T(8,128)(2,1)S(1)} %bitcast.227, f32[3,1024,512,3]{2,1,3,0:T(8,128)} %fusion.138, f32[3,3,512]{2,1,0:T(4,128)S(1)} %dynamic-slice_bitcast_fusion.2, ...), kind=kOutput, calls=%fused_computation.45.clone.1 | convolution fusion | flops 622854144 | bytes 20793348 | tf_op jit(solution)/shard_map/while/body/eval_jaxpr/kgts,tkgd->skd/dot_general | solution.py:221
  518.9 13.1 %fusion.139 = (f32[3,3,512]{2,1,0:T(4,128)S(1)}, f32[3,1024,512,3]{2,1,3,0:T(8,128)}) fusion(f32[3,1024,512,3]{2,1,3,0:T(8,128)} %fusion.138, f32[3,3,512]{2,1,0:T(4,128)S(1)} %dynamic-slice_bitcast_fusion.2, pred[512,1024]{0,1:T(8,128)(4,1)S(1)} %compare_and_fusion.5, bf16[512,3,3,64]{0,3,2,1:T(8,128)(2,1)S(1)} %bitcast.228, ...), kind=kOutput, calls=%fused_computation.29.clone.1 | convolution fusion | flops 627568128 | bytes 39292932 | tf_op jit(solution)/shard_map/while/body/eval_jaxpr/tkgd,skd->kgts/dot_general | solution.py:208
  532.0 13.5 %fusion.140 = bf16[3,3,512,1024]{2,3,1,0:T(8,128)(2,1)S(1)} fusion(f32[3,1024,512,3]{2,1,3,0:T(8,128)} %get-tuple-element.415, f32[3,1024,512,3]{2,1,3,0:T(8,128)} %fusion.138, f32[3,3,512]{2,1,0:T(4,128)S(1)} %get-tuple-element.416, f32[3,3,512]{2,1,0:T(4,128)S(1)} %dynamic-slice_bitcast_fusion.2, pred[512,1024]{0,1:T(8,128)(4,1)S(1)} %compare_and_fusion.5), kind=kLoop, calls=%fused_computation.31.clone.1 | loop fusion | flops 28311552 | bytes 47747072 | tf_op jit(solution)/shard_map/while/body/eval_jaxpr/convert_element_type | solution.py:212
  564.7 9.3 %fusion.142 = f32[4,1024,3,64]{1,3,2,0:T(8,128)} fusion(f32[4,1024,3,64]{1,3,2,0:T(8,128)} %get-tuple-element.467, s32[]{:T(128)S(6)} %copy.82, bf16[512,3,3,64]{0,3,2,1:T(8,128)(2,1)S(1)} %bitcast.227, f32[3,1024,512,3]{2,1,3,0:T(8,128)} %fusion.138, f32[3,3,512]{2,1,0:T(4,128)S(1)} %dynamic-slice_bitcast_fusion.2, ...), kind=kOutput, calls=%fused_computation.45.clone.1 | convolution fusion | flops 622854144 | bytes 20793348 | tf_op jit(solution)/shard_map/while/body/eval_jaxpr/kgts,tkgd->skd/dot_general | solution.py:221
  573.9 13.1 %fusion.139 = (f32[3,3,512]{2,1,0:T(4,128)S(1)}, f32[3,1024,512,3]{2,1,3,0:T(8,128)}) fusion(f32[3,1024,512,3]{2,1,3,0:T(8,128)} %fusion.138, f32[3,3,512]{2,1,0:T(4,128)S(1)} %dynamic-slice_bitcast_fusion.2, pred[512,1024]{0,1:T(8,128)(4,1)S(1)} %compare_and_fusion.5, bf16[512,3,3,64]{0,3,2,1:T(8,128)(2,1)S(1)} %bitcast.228, ...), kind=kOutput, calls=%fused_computation.29.clone.1 | convolution fusion | flops 627568128 | bytes 39292932 | tf_op jit(solution)/shard_map/while/body/eval_jaxpr/tkgd,skd->kgts/dot_general | solution.py:208
  587.0 13.5 %fusion.140 = bf16[3,3,512,1024]{2,3,1,0:T(8,128)(2,1)S(1)} fusion(f32[3,1024,512,3]{2,1,3,0:T(8,128)} %get-tuple-element.415, f32[3,1024,512,3]{2,1,3,0:T(8,128)} %fusion.138, f32[3,3,512]{2,1,0:T(4,128)S(1)} %get-tuple-element.416, f32[3,3,512]{2,1,0:T(4,128)S(1)} %dynamic-slice_bitcast_fusion.2, pred[512,1024]{0,1:T(8,128)(4,1)S(1)} %compare_and_fusion.5), kind=kLoop, calls=%fused_computation.31.clone.1 | loop fusion | flops 28311552 | bytes 47747072 | tf_op jit(solution)/shard_map/while/body/eval_jaxpr/convert_element_type | solution.py:212
  650.9 11.1 %add_convert_fusion.2 = bf16[4,512,576]{1,2,0:T(8,128)(2,1)} fusion(f32[4,512,576]{1,2,0:T(8,128)} %get-tuple-element.266, bf16[4,512,1536]{2,1,0:T(8,128)(2,1)} %get-tuple-element.250, bf16[1536,576]{1,0:T(8,128)(2,1)} %copy-done.10), kind=kOutput, calls=%fused_computation.94 | convolution fusion | flops 3626237952 | bytes 15138816 | tf_op jit(solution)/shard_map/gvc,cr->gvr/dot_general | solution.py:162
  666.9 40.9 %all-reduce.14 = f32[1152]{0:T(1024)S(1)} all-reduce(f32[1152]{0:T(1024)S(1)} %pad_maximum_fusion.8), channel_id=6, replica_groups=mesh['fsdp'=16,'seq'=2] {'fsdp'}, use_global_device_ids=true, to_apply=%region_18.19.clone | all-reduce | flops 1152 | bytes 9216
  717.7 181.2 %all-reduce.18.cloned.1.call-done = (f32[552960]{0:T(1024)}, f32[331776]{0:T(1024)}, f32[1769472]{0:T(1024)}, f32[884736]{0:T(1024)}) async-done(((f32[552960]{0:T(1024)}, f32[331776]{0:T(1024)}, f32[1769472]{0:T(1024)}, f32[884736]{0:T(1024)}), (f32[552960]{0:T(1024)}, f32[331776]{0:T(1024)}, f32[1769472]{0:T(1024)}, f32[884736]{0:T(1024)})) %all-reduce.18.cloned.1.call-update) | async-done | bytes 14155792
  (235 shorter events, 266.5 us)
Async XLA Ops:
  7.2 98.6 %all-gather.10.cloned.1.call-start = ((), (), s32[]{:S(2)}) async-start(), calls=%async_computation.2 | async-start | bytes 2280960 | tf_op jit(solution)/shard_map/all_gather | solution.py:74
  8.7 270.7 %all-gather.8.cloned.1.call-start = ((), (), s32[]{:S(2)}) async-start(), calls=%async_computation.1 | async-start | bytes 1824768 | tf_op jit(solution)/shard_map/all_gather | solution.py:77
  9.4 273.2 %all-gather.6.cloned.1.call-start = ((), (), s32[]{:S(2)}) async-start(), calls=%async_computation | async-start | bytes 3649536 | tf_op jit(solution)/shard_map/all_gather | solution.py:76
  10.2 888.7 %all-reduce.18.cloned.1.call-start = ((), (), s32[]{:S(2)}) async-start(), calls=%async_computation.3 | async-start | bytes 28311552
  57.5 57.9 %copy-start.29 = (f32[576]{0:T(1024)}, f32[576]{0:T(1024)S(1)}, u32[]{:S(2)}) copy-start(f32[576]{0:T(1024)S(1)} %get-tuple-element.260) | copy-start | bytes 6916
  57.5 58.0 %copy-start.2 = (bf16[4,512,576]{1,2,0:T(8,128)(2,1)S(1)}, bf16[4,512,576]{1,2,0:T(8,128)(2,1)}, u32[]{:S(2)}) copy-start(bf16[4,512,576]{1,2,0:T(8,128)(2,1)} %param.12) | copy-start | bytes 7077892
  60.4 60.2 %copy-start.24 = (f32[4,512]{1,0:T(4,128)}, f32[4,512]{1,0:T(4,128)S(1)}, u32[]{:S(2)}) copy-start(f32[4,512]{1,0:T(4,128)S(1)} %fusion.79) | copy-start | bytes 24580
  105.8 33.2 %copy-start.13 = (f32[512,32]{0,1:T(8,128)}, f32[512,32]{0,1:T(8,128)S(1)}, u32[]{:S(2)}) copy-start(f32[512,32]{0,1:T(8,128)S(1)} %get-tuple-element.261) | copy-start | bytes 196612
  120.6 6.7 copy-start.15
  120.6 10.5 %copy-start.23 = (s32[4,1024]{1,0:T(4,128)S(1)}, s32[4,1024]{1,0:T(4,128)}, u32[]{:S(2)}) copy-start(s32[4,1024]{1,0:T(4,128)} %param.13) | copy-start | bytes 49156
  120.7 10.5 %copy-start.4 = (bf16[32,1,10368]{2,1,0:T(2,128)(2,1)S(1)}, bf16[32,1,10368]{2,1,0:T(2,128)(2,1)}, u32[]{:S(2)}) copy-start(bf16[32,1,10368]{2,1,0:T(2,128)(2,1)} %all-gather.1) | copy-start | bytes 1990660
  124.2 19.6 %collective-permute-start = (bf16[4,512,3,64]{1,3,2,0:T(8,128)(2,1)}, bf16[4,512,3,64]{1,3,2,0:T(8,128)(2,1)}, u32[]{:S(2)}, u32[]{:S(2)}) collective-permute-start(bf16[4,512,3,64]{1,3,2,0:T(8,128)(2,1)} %bitcast.1), channel_id=1, source_target_pairs={{0,1},{2,3},{4,5},{6,7},{8,9},{10,11},{12,13},{14,15},{16,17},{18,... | collective-permute-start | bytes 2359304 | tf_op jit(solution)/shard_map/ppermute | solution.py:21
  128.5 18.0 %collective-permute-start.1 = (bf16[4,512,3,64]{1,3,2,0:T(8,128)(2,1)}, bf16[4,512,3,64]{1,3,2,0:T(8,128)(2,1)}, u32[]{:S(2)}, u32[]{:S(2)}) collective-permute-start(bf16[4,512,3,64]{1,3,2,0:T(8,128)(2,1)} %pad_maximum_fusion.7), channel_id=1, source_target_pairs={{0,1},{2,3},{4,5},{6,7},{8,9},{10,11},{12,13},{14,15},{16,17},{18,... | collective-permute-start | bytes 2359304 | tf_op jit(solution)/shard_map/ppermute | solution.py:21
  147.8 123.8 %copy-start.19 = (bf16[576,576]{1,0:T(8,128)(2,1)S(1)}, bf16[576,576]{1,0:T(8,128)(2,1)}, u32[]{:S(2)}) copy-start(bf16[576,576]{1,0:T(8,128)(2,1)} %reshape.216) | copy-start | bytes 1990660
  271.6 7.1 copy-start.20
  282.6 25.1 %copy-start.10 = (bf16[1536,576]{1,0:T(8,128)(2,1)}, bf16[1536,576]{1,0:T(8,128)(2,1)S(1)}, u32[]{:S(2)}) copy-start(bf16[1536,576]{1,0:T(8,128)(2,1)S(1)} %reshape.218) | copy-start | bytes 5308420
  289.9 17.8 %copy-start.8 = (bf16[4,512,576]{1,2,0:T(8,128)(2,1)S(1)}, bf16[4,512,576]{1,2,0:T(8,128)(2,1)}, u32[]{:S(2)}) copy-start(bf16[4,512,576]{1,2,0:T(8,128)(2,1)} %param.19) | copy-start | bytes 7077892
  331.4 20.8 %copy-start.26 = (f32[4,512]{1,0:T(4,128)S(1)}, f32[4,512]{1,0:T(4,128)}, u32[]{:S(2)}) copy-start(f32[4,512]{1,0:T(4,128)} %fusion.80) | copy-start | bytes 24580
  331.4 20.8 %copy-start.31 = (f32[576]{0:T(1024)S(1)}, f32[576]{0:T(1024)}, u32[]{:S(2)}) copy-start(f32[576]{0:T(1024)} %get-tuple-element.259) | copy-start | bytes 6916
  368.5 9.4 %copy-start.28 = (f32[4,512]{1,0:T(4,128)S(1)}, f32[4,512]{1,0:T(4,128)}, u32[]{:S(2)}) copy-start(f32[4,512]{1,0:T(4,128)} %copy-done.27) | copy-start | bytes 24580
  368.5 9.4 %copy-start.5 = (f32[4,512,576]{1,2,0:T(8,128)S(1)}, f32[4,512,576]{1,2,0:T(8,128)}, u32[]{:S(2)}) copy-start(f32[4,512,576]{1,2,0:T(8,128)} %get-tuple-element.267) | copy-start | bytes 14155780
  368.5 9.4 %copy-start.9 = (bf16[4,512,576]{1,2,0:T(8,128)(2,1)S(1)}, bf16[4,512,576]{1,2,0:T(8,128)(2,1)}, u32[]{:S(2)}) copy-start(bf16[4,512,576]{1,2,0:T(8,128)(2,1)} %param.19) | copy-start | bytes 7077892
  377.9 6.1 copy-start.18
  608.8 27.6 %collective-permute-start.2 = (bf16[4,512,3,64]{1,3,2,0:T(8,128)(2,1)S(1)}, bf16[4,512,3,64]{1,3,2,0:T(8,128)(2,1)S(1)}, u32[]{:S(2)}, u32[]{:S(2)}) collective-permute-start(bf16[4,512,3,64]{1,3,2,0:T(8,128)(2,1)S(1)} %slice.105), channel_id=1, source_target_pairs={{1,0},{3,2},{5,4},{7,6},{9,8},{11,10},{13,12},{15,14},{17,16},{19,... | collective-permute-start | bytes 2359304 | tf_op jit(solution)/shard_map/ppermute | solution.py:21
  620.7 12.0 %copy-start.14 = (f32[512,32]{0,1:T(8,128)S(1)}, f32[512,32]{0,1:T(8,128)}, u32[]{:S(2)}) copy-start(f32[512,32]{0,1:T(8,128)} %copy-done.13) | copy-start | bytes 196612
  620.7 12.0 %copy-start.16 = (f32[512,32]{0,1:T(8,128)S(1)}, f32[512,32]{0,1:T(8,128)}, u32[]{:S(2)}) copy-start(f32[512,32]{0,1:T(8,128)} %get-tuple-element.262) | copy-start | bytes 196612
  631.4 7.5 collective-permute-start.3
  638.4 3.8 copy-start.3
  650.9 11.2 %copy-start.7 = (bf16[4,512,768]{1,2,0:T(8,128)(2,1)S(1)}, bf16[4,512,768]{1,2,0:T(8,128)(2,1)}, u32[]{:S(2)}) copy-start(bf16[4,512,768]{1,2,0:T(8,128)(2,1)} %copy-done.6) | copy-start | bytes 9437188
  650.9 11.2 %copy-start.17 = (bf16[576,960,1]{1,0,2:T(8,128)(2,1)S(1)}, bf16[576,960,1]{1,0,2:T(8,128)(2,1)}, u32[]{:S(2)}) copy-start(bf16[576,960,1]{1,0,2:T(8,128)(2,1)} %reshape.246) | copy-start | bytes 3317764
  662.0 4.8 copy-start.32
  662.0 48.8 %copy-start.22 = (f32[4,512]{1,0:T(4,128)S(1)}, f32[4,512]{1,0:T(4,128)}, u32[]{:S(2)}) copy-start(f32[4,512]{1,0:T(4,128)} %copy-done.21) | copy-start | bytes 24580
  (10 other events, 24.5 us)
Sparse Core Ops, SparseCore 0:
  11.5 60.3 all-gather.9
  74.7 55.2 all-gather.7
  132.9 59.6 all-gather.5
  650.3 248.5 all-reduce.17
where the time goes:
time: 923 us; the launch traced here: 912 us
  matrix products  340 us (37%)
  waiting for transfers between devices  183 us (20%)
  other arithmetic  144 us (16%)
  blocking collectives  131 us (14%)
  local copies, waits for them, and re-layouts  88.6 us (10%)
  between operations  16.1 us (2%)
    unnamed x5, waiting for transfers between devices  183 us
    unnamed x2, blocking collectives  84.5 us
    dot_general x8, matrix products, scores_of(): jnp.einsum('tkgd,skd->kgts', grouped, key, preferred_element_type=jnp.flo...  63.5 us
    convert_element_type x4, other arithmetic, backward_one(): delta_scores = (probs * (delta_probs - row_dot)).astype(jnp.bfloat16)  53.9 us
    dot_general x4, matrix products, backward_one(): jnp.einsum('tkgd,skd->kgts', delta_grouped, value, preferred_element_type...  52.3 us
    all_gather x1, blocking collectives, per_device(): lax.all_gather(output_weight, ('fsdp', 'seq'), axis=0, tiled=True)  43.7 us
    reduce_sum x4, other arithmetic, forward_one(): total = jnp.sum(powers, axis=-1, keepdims=True)  41 us
    dot_general x4, matrix products, backward_one(): jnp.einsum('kgts,tkgd->skd', probs.astype(jnp.bfloat16), delta_grouped, p...  37 us
  transfers between devices with their start and end apart: 8, of which 1 were waited for; matrix products, arithmetic and copies ran while one was open for 24% of the time, Pallas kernels for 0%

commit v1 on v0

v1 whole, which is shorter than its diff:
```python
import jax
import jax.numpy as jnp
from jax import lax
from jax.experimental import pallas as pl
from jax.experimental.pallas import tpu as pltpu
from jax.sharding import PartitionSpec as P

D = 576
H = 9
KV = 3
HD = 64
FF = 1536
GROUP = H // KV
ROWS = 128

EPSILON = 1e-05
THETA = 100000.0
MASKED = -1e30
VMEM_LIMIT = 48 * 1024 * 1024


def root_norm(values, gain):
    return values * lax.rsqrt(jnp.mean(values * values, axis=-1, keepdims=True) + EPSILON) * gain


def gated_unit(gate_up_activations):
    middle = gate_up_activations.shape[-1] // 2
    return jax.nn.silu(gate_up_activations[..., :middle]) * gate_up_activations[..., middle:]


def shifted(block, axis, distance):
    devices = range(lax.axis_size(axis))
    route = [(i - distance, i) for i in devices if i - distance in devices]
    return lax.ppermute(block, axis, route)


def halved(block, axis, bit):
    size = lax.axis_size(axis)
    mine = (lax.axis_index(axis) // bit) % 2
    low = block.astype(jnp.bfloat16)
    away = lax.dynamic_index_in_dim(low, 1 - mine, axis=1, keepdims=False)
    kept = lax.dynamic_index_in_dim(block, mine, axis=1, keepdims=False)
    came = lax.ppermute(away, axis, [(i, i ^ bit) for i in range(size)])
    return kept.astype(jnp.float32) + came.astype(jnp.float32)


def reduce_scatter(parts, shards, halves):
    sizes = [part.shape[-1] for part in parts]
    total = sum(sizes)
    padded = -(-total // 128) * 128
    joined = jnp.concatenate([part.astype(jnp.bfloat16) for part in parts], axis=-1)
    joined = jnp.pad(joined, ((0, 0), (0, 0), (0, padded - total)))
    block = joined.reshape(shards, halves, padded // 128, 128)
    block = halved(block, "seq", 1)
    bit = 1
    while bit < shards:
        block = halved(block.reshape(-1, 2, padded // 128, 128), "fsdp", bit)
        bit *= 2
    flat = block.reshape(-1)
    outs, at = [], 0
    for size in sizes:
        outs.append(flat[at : at + size])
        at += size
    return outs


def project_kernel(x_ref, gain_ref, weight_ref, cos_ref, sin_ref, normed_ref, queries_ref, kv_ref):
    x = x_ref[0].astype(jnp.float32)
    normed = root_norm(x, gain_ref[...]).astype(jnp.bfloat16)
    normed_ref[0] = normed
    projected = lax.dot_general(
        weight_ref[...], normed, (((1,), (1,)), ((), ())), preferred_element_type=jnp.float32
    )
    cos = cos_ref[...]
    sin = sin_ref[...]
    keys = []
    for head in range(H + KV):
        first = projected[head * HD : head * HD + 32]
        second = projected[head * HD + 32 : (head + 1) * HD]
        turned = jnp.concatenate([first * cos - second * sin, second * cos + first * sin], axis=0)
        if head < H:
            low = turned.astype(jnp.bfloat16).astype(jnp.float32) * HD ** (-0.5)
            queries_ref[0, head * HD : (head + 1) * HD, :] = low.astype(jnp.bfloat16)
        else:
            keys.append(turned)
    both = jnp.concatenate(keys + [projected[(H + KV) * HD :]], axis=0)
    kv_ref[0] = both.T.astype(jnp.bfloat16)


def project(x, gain, weight_t, cos, sin):
    count, half = x.shape[0], x.shape[1]
    wide = (H + 2 * KV) * HD
    return pl.pallas_call(
        project_kernel,
        grid=(count,),
        in_specs=[
            pl.BlockSpec((1, half, D), lambda i: (i, 0, 0)),
            pl.BlockSpec((1, D), lambda i: (0, 0)),
            pl.BlockSpec((wide, D), lambda i: (0, 0)),
            pl.BlockSpec((32, half), lambda i: (0, 0)),
            pl.BlockSpec((32, half), lambda i: (0, 0)),
        ],
        out_specs=[
            pl.BlockSpec((1, half, D), lambda i: (i, 0, 0)),
            pl.BlockSpec((1, H * HD, half), lambda i: (i, 0, 0)),
            pl.BlockSpec((1, half, 2 * KV * HD), lambda i: (i, 0, 0)),
        ],
        out_shape=[
            jax.ShapeDtypeStruct((count, half, D), jnp.bfloat16),
            jax.ShapeDtypeStruct((count, H * HD, half), jnp.bfloat16),
            jax.ShapeDtypeStruct((count, half, 2 * KV * HD), jnp.bfloat16),
        ],
        compiler_params=pltpu.CompilerParams(vmem_limit_bytes=VMEM_LIMIT),
        cost_estimate=pl.CostEstimate(
            flops=2 * count * half * D * wide, bytes_accessed=count * half * 4096, transcendentals=0
        ),
    )(x, gain, weight_t, cos, sin)


WIDTHS = (1, 2, 3, 4, 5, 6, 8)


def load_window(far_ref, near_ref, labels_ref, keys, values, key_labels):
    half = near_ref.shape[1]
    for group in range(KV):
        at = slice(group * HD, (group + 1) * HD)
        later = slice((KV + group) * HD, (KV + group + 1) * HD)
        keys[group, :half, :] = far_ref[0, :, at]
        keys[group, half:, :] = near_ref[0, :, at]
        values[group, :half, :] = far_ref[0, :, later]
        values[group, half:, :] = near_ref[0, :, later]
    key_labels[...] = jnp.broadcast_to(labels_ref[0], (ROWS, 2 * half)).T


def window_bias(width, start, query_start, labels_ref, key_labels):
    query_row = labels_ref[0, :, pl.ds(query_start, ROWS)]
    same = key_labels[pl.ds(start, width * ROWS), :] == query_row
    shape = (width * ROWS, ROWS)
    key_place = lax.broadcasted_iota(jnp.int32, shape, 0) + start
    query_place = lax.broadcasted_iota(jnp.int32, shape, 1) + query_start
    bias = jnp.where(same & (key_place <= query_place), 0.0, MASKED)
    return jnp.concatenate([bias] * GROUP, axis=1)


def side_by_side(block, group):
    return jnp.concatenate(
        [block[(group * GROUP + i) * HD : (group * GROUP + i + 1) * HD] for i in range(GROUP)], axis=1
    )


def over_widths(first_ref, body):
    block = pl.program_id(1)
    blocks = pl.num_programs(1)
    diagonal = blocks + block
    need = diagonal + 1 - first_ref[pl.program_id(0), block]
    below = 0
    for width in WIDTHS:
        if width > 8:
            continue

        @pl.when((need > below) & (need <= width))
        def _(width=width):
            start = jnp.maximum(diagonal + 1 - width, 0) * ROWS
            body(width, pl.multiple_of(start, ROWS))

        below = width


def forward_kernel(
    first_ref, queries_ref, far_ref, near_ref, labels_ref, mixed_ref, log_ref, keys, values, key_labels, mixed_t
):
    @pl.when(pl.program_id(1) == 0)
    def _():
        load_window(far_ref, near_ref, labels_ref, keys, values, key_labels)

    query_start = pl.multiple_of(near_ref.shape[1] + pl.program_id(1) * ROWS, ROWS)

    def body(width, start):
        bias = window_bias(width, start, query_start, labels_ref, key_labels)
        queries = queries_ref[0]
        window = pl.ds(start, width * ROWS)
        for group in range(KV):
            scores = jnp.dot(
                keys[group, window, :], side_by_side(queries, group), preferred_element_type=jnp.float32
            )
            scores = scores + bias
            top = jnp.max(scores, axis=0, keepdims=True)
            powers = jnp.exp(scores - top)
            total = jnp.sum(powers, axis=0, keepdims=True)
            weights = (powers * (1.0 / total)).astype(jnp.bfloat16)
            out = lax.dot_general(
                values[group, window, :], weights, (((0,), (0,)), ((), ())), preferred_element_type=jnp.float32
            )
            log_ref[0, 0, group : group + 1, :] = top + jnp.log(total)
            for i in range(GROUP):
                head = group * GROUP + i
                mixed_t[head * HD : (head + 1) * HD, :] = out[:, i * ROWS : (i + 1) * ROWS]

    over_widths(first_ref, body)
    mixed_ref[0] = mixed_t[...].T.astype(jnp.bfloat16)


def attention_forward(first, queries, far, near, labels):
    count, half = near.shape[0], near.shape[1]
    blocks = half // ROWS
    wide = 2 * KV * HD
    grid_spec = pltpu.PrefetchScalarGridSpec(
        num_scalar_prefetch=1,
        grid=(count, blocks),
        in_specs=[
            pl.BlockSpec((1, H * HD, ROWS), lambda i, j, s: (i, 0, j)),
            pl.BlockSpec((1, half, wide), lambda i, j, s: (i, 0, 0)),
            pl.BlockSpec((1, half, wide), lambda i, j, s: (i, 0, 0)),
            pl.BlockSpec((1, 1, 2 * half), lambda i, j, s: (i, 0, 0)),
        ],
        out_specs=[
            pl.BlockSpec((1, ROWS, H * HD), lambda i, j, s: (i, j, 0)),
            pl.BlockSpec((1, 1, 8, GROUP * ROWS), lambda i, j, s: (i, j, 0, 0)),
        ],
        scratch_shapes=[
            pltpu.VMEM((KV, 2 * half, HD), jnp.bfloat16),
            pltpu.VMEM((KV, 2 * half, HD), jnp.bfloat16),
            pltpu.VMEM((2 * half, ROWS), jnp.float32),
            pltpu.VMEM((H * HD, ROWS), jnp.float32),
        ],
    )
    return pl.pallas_call(
        forward_kernel,
        grid_spec=grid_spec,
        out_shape=[
            jax.ShapeDtypeStruct((count, half, H * HD), jnp.bfloat16),
            jax.ShapeDtypeStruct((count, blocks, 8, GROUP * ROWS), jnp.float32),
        ],
        compiler_params=pltpu.CompilerParams(vmem_limit_bytes=VMEM_LIMIT),
        cost_estimate=pl.CostEstimate(
            flops=count * H * half * half * HD * 16, bytes_accessed=count * half * 4096, transcendentals=0
        ),
    )(first, queries, far, near, labels)


def backward_kernel(
    first_ref, queries_ref, delta_ref, log_ref, far_ref, near_ref, labels_ref, cos_ref, sin_ref,
    delta_queries_ref, delta_far_ref, delta_near_ref,
    keys, values, key_labels, turned_t, sums,
):
    half = near_ref.shape[1]
    block = pl.program_id(1)

    @pl.when(block == 0)
    def _():
        load_window(far_ref, near_ref, labels_ref, keys, values, key_labels)
        sums[...] = jnp.zeros_like(sums)

    query_start = pl.multiple_of(half + block * ROWS, ROWS)

    def body(width, start):
        bias = window_bias(width, start, query_start, labels_ref, key_labels)
        queries = queries_ref[0]
        deltas = delta_ref[0].astype(jnp.float32).T.astype(jnp.bfloat16)
        window = pl.ds(start, width * ROWS)
        cos = cos_ref[:, pl.ds(query_start, ROWS)]
        sin = sin_ref[:, pl.ds(query_start, ROWS)]
        for group in range(KV):
            key = keys[group, window, :]
            query = side_by_side(queries, group)
            delta = side_by_side(deltas, group)
            scores = jnp.dot(key, query, preferred_element_type=jnp.float32) + bias
            probs = jnp.exp(scores - log_ref[0, 0, group : group + 1, :])
            delta_probs = jnp.dot(values[group, window, :], delta, preferred_element_type=jnp.float32)
            row_dot = jnp.sum(probs * delta_probs, axis=0, keepdims=True)
            delta_scores = (probs * (delta_probs - row_dot)).astype(jnp.bfloat16)
            out = lax.dot_general(
                key, delta_scores, (((0,), (0,)), ((), ())), preferred_element_type=jnp.float32
            ) * HD ** (-0.5)
            sums[group, window, :] += lax.dot_general(
                delta_scores, query, (((1,), (1,)), ((), ())), preferred_element_type=jnp.float32
            )
            sums[KV + group, window, :] += lax.dot_general(
                probs.astype(jnp.bfloat16), delta, (((1,), (1,)), ((), ())), preferred_element_type=jnp.float32
            )
            for i in range(GROUP):
                at = (group * GROUP + i) * HD
                first = out[:32, i * ROWS : (i + 1) * ROWS]
                second = out[32:, i * ROWS : (i + 1) * ROWS]
                turned_t[at : at + 32, :] = first * cos + second * sin
                turned_t[at + 32 : at + HD, :] = second * cos - first * sin

    over_widths(first_ref, body)
    delta_queries_ref[0] = turned_t[...].T.astype(jnp.bfloat16)

    @pl.when(block == pl.num_programs(1) - 1)
    def _():
        pieces = []
        for group in range(KV):
            flipped = sums[group].T
            first, second = flipped[:32], flipped[32:]
            pieces.append(first * cos_ref[...] + second * sin_ref[...])
            pieces.append(second * cos_ref[...] - first * sin_ref[...])
        key_sums = jnp.concatenate(pieces, axis=0).T
        value_sums = jnp.concatenate([sums[KV + group] for group in range(KV)], axis=1)
        wide = KV * HD
        delta_far_ref[0, :, :wide] = key_sums[:half].astype(jnp.bfloat16)
        delta_far_ref[0, :, wide:] = value_sums[:half].astype(jnp.bfloat16)
        delta_near_ref[0, :, :wide] = key_sums[half:]
        delta_near_ref[0, :, wide:] = value_sums[half:]


def attention_backward(first, queries, delta_mixed, logs, far, near, labels, cos, sin):
    count, half = near.shape[0], near.shape[1]
    blocks = half // ROWS
    wide = 2 * KV * HD
    grid_spec = pltpu.PrefetchScalarGridSpec(
        num_scalar_prefetch=1,
        grid=(count, blocks),
        in_specs=[
            pl.BlockSpec((1, H * HD, ROWS), lambda i, j, s: (i, 0, j)),
            pl.BlockSpec((1, ROWS, H * HD), lambda i, j, s: (i, j, 0)),
            pl.BlockSpec((1, 1, 8, GROUP * ROWS), lambda i, j, s: (i, j, 0, 0)),
            pl.BlockSpec((1, half, wide), lambda i, j, s: (i, 0, 0)),
            pl.BlockSpec((1, half, wide), lambda i, j, s: (i, 0, 0)),
            pl.BlockSpec((1, 1, 2 * half), lambda i, j, s: (i, 0, 0)),
            pl.BlockSpec((32, 2 * half), lambda i, j, s: (0, 0)),
            pl.BlockSpec((32, 2 * half), lambda i, j, s: (0, 0)),
        ],
        out_specs=[
            pl.BlockSpec((1, ROWS, H * HD), lambda i, j, s: (i, j, 0)),
            pl.BlockSpec((1, half, wide), lambda i, j, s: (i, 0, 0)),
            pl.BlockSpec((1, half, wide), lambda i, j, s: (i, 0, 0)),
        ],
        scratch_shapes=[
            pltpu.VMEM((KV, 2 * half, HD), jnp.bfloat16),
            pltpu.VMEM((KV, 2 * half, HD), jnp.bfloat16),
            pltpu.VMEM((2 * half, ROWS), jnp.float32),
            pltpu.VMEM((H * HD, ROWS), jnp.float32),
            pltpu.VMEM((2 * KV, 2 * half, HD), jnp.float32),
        ],
    )
    return pl.pallas_call(
        backward_kernel,
        grid_spec=grid_spec,
        out_shape=[
            jax.ShapeDtypeStruct((count, half, H * HD), jnp.bfloat16),
            jax.ShapeDtypeStruct((count, half, wide), jnp.bfloat16),
            jax.ShapeDtypeStruct((count, half, wide), jnp.float32),
        ],
        compiler_params=pltpu.CompilerParams(vmem_limit_bytes=VMEM_LIMIT),
        cost_estimate=pl.CostEstimate(
            flops=count * H * half * half * HD * 40, bytes_accessed=count * half * 8192, transcendentals=0
        ),
    )(first, queries, delta_mixed, logs, far, near, labels, cos, sin)


def per_device(
    layer_input,
    segments,
    project_weight,
    output_weight,
    gate_up_weight,
    down_weight,
    gains,
    cotangent,
):
    sequences, half = layer_input.shape[0], layer_input.shape[1]
    shards, halves = lax.axis_size("fsdp"), lax.axis_size("seq")
    both = ("fsdp", "seq")

    cut, own = project_weight.shape[0], gains.shape[0]
    fill = jnp.zeros((-(cut + own) % 128,), gains.dtype)
    early = lax.all_gather(jnp.concatenate([project_weight, gains, fill]), both, axis=0, tiled=True)
    early = early.reshape(shards * halves, -1)
    project_matrix = early[:, :cut].reshape(D, (H + 2 * KV) * HD)
    gain_whole = early[::halves, cut : cut + own].reshape(2 * D).astype(jnp.float32)
    output_matrix = lax.all_gather(output_weight, both, axis=0, tiled=True).reshape(H * HD, D)
    gate_up_matrix = lax.all_gather(gate_up_weight, both, axis=0, tiled=True).reshape(D, 2 * FF)
    down_matrix = lax.all_gather(down_weight, both, axis=0, tiled=True).reshape(FF, D)

    start = lax.axis_index("seq") * half
    places = start - half + jnp.arange(2 * half, dtype=jnp.int32)
    rates = THETA ** (-(jnp.arange(HD // 2, dtype=jnp.float32) * 2.0) / HD)
    angle = rates[:, None] * places.astype(jnp.float32)[None, :]
    cos, sin = jnp.cos(angle), jnp.sin(angle)
    padded = jnp.concatenate([jnp.full((sequences, half), -1, jnp.int32), segments], axis=1)
    key_labels = lax.dynamic_slice_in_dim(padded, start, 2 * half, axis=1)
    block_labels = key_labels[:, half::ROWS]
    first = (
        jnp.sum((key_labels[:, None, :] < block_labels[:, :, None]).astype(jnp.int32), axis=-1) // ROWS
    )
    labels = key_labels.astype(jnp.float32)[:, None, :]

    normed, queries, near = project(
        layer_input, gain_whole[None, :D], project_matrix.T, cos[:, half:], sin[:, half:]
    )
    far = shifted(near, "seq", 1)
    mixed, logs = attention_forward(first, queries, far, near, labels)

    hidden_features = layer_input.astype(jnp.float32)
    residual_stream = hidden_features + jnp.einsum(
        "crz,zm->crm", mixed, output_matrix, preferred_element_type=jnp.float32
    )
    mixer_input = root_norm(residual_stream, gain_whole[D:]).astype(jnp.bfloat16)
    gate_up_activations = jnp.einsum(
        "mar,rw->maw", mixer_input, gate_up_matrix, preferred_element_type=jnp.float32
    )
    hidden_state, unit_pull = jax.vjp(gated_unit, gate_up_activations)
    hidden_low = hidden_state.astype(jnp.bfloat16)
    result = (
        residual_stream
        + jnp.einsum("gvc,cr->gvr", hidden_low, down_matrix, preferred_element_type=jnp.float32)
    ).astype(jnp.bfloat16)
    delta_down = jnp.einsum(
        "rqh,rqo->ho", hidden_low, cotangent, preferred_element_type=jnp.float32
    )
    delta_hidden = jnp.einsum(
        "iou,eu->ioe", cotangent, down_matrix, preferred_element_type=jnp.float32
    )
    gate_up_cotangent = unit_pull(delta_hidden)[0].astype(jnp.bfloat16)
    delta_gate_up = jnp.einsum(
        "bqg,bqv->gv", mixer_input, gate_up_cotangent, preferred_element_type=jnp.float32
    )
    delta_mixer = jnp.einsum(
        "evi,ai->eva", gate_up_cotangent, gate_up_matrix, preferred_element_type=jnp.float32
    )
    mixer_pull = jax.vjp(root_norm, residual_stream, gain_whole[D:])[1]
    delta_residual, delta_gain_mixer = mixer_pull(delta_mixer)
    delta_residual = delta_residual + cotangent.astype(jnp.float32)
    branch = delta_residual.astype(jnp.bfloat16)
    delta_output = jnp.einsum("zxa,zxq->aq", mixed, branch, preferred_element_type=jnp.float32)
    delta_mixed = jnp.einsum(
        "wrc,jc->wrj", branch, output_matrix, preferred_element_type=jnp.float32
    ).astype(jnp.bfloat16)

    def spread(matrix):
        return matrix.astype(jnp.bfloat16).reshape(shards, halves, -1)

    gate_up_gradient, down_gradient, output_gradient = reduce_scatter(
        [spread(delta_gate_up), spread(delta_down), spread(delta_output)], shards, halves
    )

    pieces = []
    for i in range(sequences):
        at = slice(i, i + 1)
        pieces.append(
            attention_backward(
                first[at], queries[at], delta_mixed[at], logs[at], far[at], near[at], labels[at], cos, sin
            )
        )
    delta_queries, delta_far, delta_near = [jnp.concatenate(piece, axis=0) for piece in zip(*pieces)]
    back = shifted(delta_far, "seq", -1)
    delta_kv = (delta_near + back.astype(jnp.float32)).astype(jnp.bfloat16)
    projected_cotangent = jnp.concatenate([delta_queries, delta_kv], axis=-1)
    delta_project = jnp.einsum(
        "zgv,zgf->vf", normed, projected_cotangent, preferred_element_type=jnp.float32
    )
    delta_normed = jnp.einsum(
        "xgc,fc->xgf", projected_cotangent, project_matrix, preferred_element_type=jnp.float32
    )
    attend_pull = jax.vjp(root_norm, hidden_features, gain_whole[:D])[1]
    delta_features, delta_gain_attend = attend_pull(delta_normed)
    input_gradient = (delta_residual + delta_features).astype(jnp.bfloat16)
    delta_gain = jnp.concatenate([delta_gain_attend, delta_gain_mixer]).reshape(shards, 1, -1)
    project_gradient, gains_gradient = reduce_scatter(
        [spread(delta_project), jnp.broadcast_to(delta_gain, (shards, halves, delta_gain.shape[-1]))],
        shards,
        halves,
    )
    return (
        result,
        input_gradient,
        project_gradient,
        output_gradient,
        gate_up_gradient,
        down_gradient,
        gains_gradient,
    )


def solution(mesh):
    return jax.shard_map(
        per_device,
        mesh=mesh,
        in_specs=(
            P("fsdp", "seq", None),
            P("fsdp", None),
            P(("fsdp", "seq")),
            P(("fsdp", "seq")),
            P(("fsdp", "seq")),
            P(("fsdp", "seq")),
            P("fsdp"),
            P("fsdp", "seq", None),
        ),
        out_specs=(
            P("fsdp", "seq", None),
            P("fsdp", "seq", None),
            P(("fsdp", "seq")),
            P(("fsdp", "seq")),
            P(("fsdp", "seq")),
            P(("fsdp", "seq")),
            P("fsdp"),
        ),
        check_vma=False,
    )
```

time: 923 us -> 526 us (0.57)
  matrix products: 340 us -> 118 us
  other arithmetic: 144 us -> 37.4 us
  waiting for transfers between devices: 183 us -> 95.1 us
  blocking collectives: 131 us -> 50.5 us
  Pallas kernels: 0 us -> 75 us
  starting transfers between devices: 8.51 us -> 36.9 us
    dot_general x39 -> x10, matrix products: 320 us -> 102 us  [the longest x1 23.7 us: per_device(): jnp.einsum('iou,eu->ioe', cotangent, down_matrix, preferred_element_type=...]
    unnamed x5 -> x3, waiting for transfers between devices: 183 us -> 1.39 us
    unnamed x2 -> x0, blocking collectives: 84.5 us -> none
    pallas_call x0 -> x6, Pallas kernels: none -> 75 us  [the longest x4 41.6 us: attention_backward(): pl.pallas_call(backward_kernel, grid_spec=grid_spec, out_shape=[jax.Shape...]
    convert_element_type x6 -> x4, other arithmetic: 54.5 us -> 2.61 us  [the longest x1 1.89 us: per_device(): delta_kv = (delta_near + back.astype(jnp.float32)).astype(jnp.bfloat16)]
    ppermute x0 -> x10, waiting for transfers between devices: none -> 51.3 us  [halved(): came = lax.ppermute(away, axis, [(i, i ^ bit) for i in range(size)])]
    all_gather x3, waiting for transfers between devices: 0.02 us -> 42.4 us  [the longest x1 21.6 us: per_device(): lax.all_gather(gate_up_weight, both, axis=0, tiled=True).reshape(D, 2 * FF)]
    reduce_sum x4 -> x1, other arithmetic: 41 us -> 0.22 us  [per_device(): jnp.sum((key_labels[:, None, :] < block_labels[:, :, None]).astype(jnp.in...]
  transfers between devices with their start and end apart: 8 -> 15, of which waited for: 1 -> 10; matrix products, arithmetic and copies ran while one was open for 24% -> 19% of each run, Pallas kernels for 0% -> 6%
where the time goes in v1:
time: 526 us; the launch traced here: 522 us
  matrix products  118 us (22%)
  waiting for transfers between devices  95.1 us (18%)
  local copies, waits for them, and re-layouts  93.6 us (18%)
  Pallas kernels  75 us (14%)
  blocking collectives  50.5 us (10%)
  other arithmetic  37.4 us (7%)
  starting transfers between devices  36.9 us (7%)
  between operations  15.2 us (3%)
    ppermute x10, waiting for transfers between devices, halved(): came = lax.ppermute(away, axis, [(i, i ^ bit) for i in range(size)])  51.3 us
    all_gather x1, blocking collectives, per_device(): lax.all_gather(output_weight, both, axis=0, tiled=True).reshape(H * HD, D)  50.5 us
    pallas_call x4, Pallas kernels, attention_backward(): pl.pallas_call(backward_kernel, grid_spec=grid_spec, out_shape=[jax.Shape...  41.6 us
    ppermute x10, starting transfers between devices, halved(): came = lax.ppermute(away, axis, [(i, i ^ bit) for i in range(size)])  31.8 us
    pallas_call x1, Pallas kernels, attention_forward(): pl.pallas_call(forward_kernel, grid_spec=grid_spec, out_shape=[jax.ShapeD...  26.2 us
    reshape x7, local copies, waits for them, and re-layouts, spread(): return matrix.astype(jnp.bfloat16).reshape(shards, halves, -1)  26.1 us
    dot_general x1, matrix products, per_device(): jnp.einsum('iou,eu->ioe', cotangent, down_matrix, preferred_element_type=...  23.7 us
    all_gather x1, waiting for transfers between devices, per_device(): lax.all_gather(gate_up_weight, both, axis=0, tiled=True).reshape(D, 2 * FF)  21.6 us
  transfers between devices with their start and end apart: 15, of which 10 were waited for; matrix products, arithmetic and copies ran while one was open for 19% of the time, Pallas kernels for 6%

profile of v1, /device:TPU:0, one launch (start us, length us, event | category | flops | bytes accessed | tf_op | source)
XLA Modules:
  0.0 522.0 jit_solution(15034252689489594402)
XLA Ops:
  17.6 50.5 %all-gather = bf16[32,1,10368]{2,1,0:T(2,128)(2,1)} all-gather(bf16[1,1,10368]{2,1,0:T(2,128)(2,1)S(1)} %reshape.180), channel_id=1, replica_groups=mesh['fsdp'=16,'seq'=2] {'fsdp','seq'}, dimensions={0}, use_global_device_ids=true | all-gather | bytes 684288 | tf_op jit(solution)/shard_map/all_gather | solution.py:373
  75.2 7.3 %shard_map.135 = (bf16[4,512,576]{2,1,0:T(8,128)(2,1)}, bf16[4,576,512]{2,1,0:T(8,128)(2,1)S(1)}, bf16[4,512,384]{2,1,0:T(8,128)(2,1)}) custom-call(bf16[4,512,576]{2,1,0:T(8,128)(2,1)} %copy.99.x_ref, f32[1,576]{1,0:T(1,128)S(1)} %broadcast_in_dim.13.gain_ref, bf16[960,576]{1,0:T(8,128)(2,1)S(1)} %bitcast.96, f32[32,512]{1,0:T(8,128)S(1)} %slice.212.cos_ref, ...), custom_call_target="tpu_custom_call" | custom-call | flops 2264924160 | bytes 8388608 | tf_op jit(solution)/shard_map/pallas_call | solution.py:93
  86.2 5.8 %reduce = bf16[32,10368]{1,0:T(8,128)(2,1)} reduce(bf16[32,1,10368]{2,1,0:T(2,128)(2,1)} %all-gather, bf16[]{:T(256)} %constant.242), dimensions={1}, to_apply=%all-gather.reduce_sub_computation | reduce | bytes 1327106 | tf_op jit(solution)/shard_map/all_gather | solution.py:373
  108.2 19.3 %all-gather.9.cloned.1.call-done = bf16[884736]{0:T(1024)(128)(2,1)} async-done(((bf16[27648]{0:T(1024)(128)(2,1)}), bf16[884736]{0:T(1024)(128)(2,1)}) %all-gather.9.cloned.1.call-update) | async-done | bytes 1769488 | tf_op jit(solution)/shard_map/all_gather | solution.py:375
  132.5 26.2 %shard_map.136 = (bf16[4,512,576]{2,1,0:T(8,128)(2,1)}, f32[4,4,8,384]{3,2,1,0:T(8,128)S(1)}) custom-call(s32[4,4]{1,0:T(4,128)S(1)} %copy-done.17, bf16[4,576,512]{2,1,0:T(8,128)(2,1)S(1)} %get-tuple-element.24.queries_ref, bf16[4,512,384]{2,1,0:T(8,128)(2,1)} %collective-permute-done.far_ref, bf16[4,512,384]{2,1,0:T(8,128)(2,1)} %get-tuple-element.25.near_ref, ...), custom_call_target="tpu_custom_call" | custom-call | flops 9663676416 | bytes 8388608 | tf_op jit(solution)/shard_map/pallas_call | solution.py:227
  158.7 6.2 %multiply_reduce_fusion.2 = (f32[4,512]{1,0:T(4,128)S(1)}, f32[4,512,576]{1,2,0:T(8,128)}) fusion(bf16[4,512,576]{2,1,0:T(8,128)(2,1)} %get-tuple-element.26, bf16[576,576]{1,0:T(8,128)(2,1)S(1)} %copy-done.49, bf16[4,512,576]{1,2,0:T(8,128)(2,1)S(1)} %copy-done.38), kind=kOutput, calls=%fused_computation.28 | convolution fusion | flops 1363671040 | bytes 10108928 | tf_op jit(solution)/shard_map/crz,zm->crm/dot_general | solution.py:397
  168.0 21.6 %all-gather.7.cloned.1.call-done = bf16[1769472]{0:T(1024)(128)(2,1)} async-done(((bf16[55296]{0:T(1024)(128)(2,1)}), bf16[1769472]{0:T(1024)(128)(2,1)}) %all-gather.7.cloned.1.call-update) | async-done | bytes 3538960 | tf_op jit(solution)/shard_map/all_gather | solution.py:374
  189.5 6.5 %reshape.184 = bf16[576,3072,1]{1,0,2:T(8,128)(2,1)} reshape(bf16[1769472]{0:T(1024)(128)(2,1)} %all-gather.7.cloned.1.call-done) | data formatting | bytes 7077888 | tf_op jit(solution)/shard_map/reshape | solution.py:374
  196.1 17.8 %fusion.34 = f32[4,512,3072]{2,1,0:T(8,128)} fusion(bf16[576,3072,1]{1,0,2:T(8,128)(2,1)} %reshape.184, f32[4,512,576]{1,2,0:T(8,128)} %get-tuple-element.83, f32[576]{0:T(1024)S(1)} %copy-done.55, f32[4,512]{1,0:T(4,128)S(1)} %fusion.27), kind=kOutput, calls=%fused_computation.106 | convolution fusion | flops 7251296256 | bytes 33433856 | tf_op jit(solution)/shard_map/mar,rw->maw/dot_general | solution.py:401
  213.9 23.7 %fusion.17 = (f32[4,512,1536]{2,1,0:T(8,128)}, f32[4,512,1536]{2,1,0:T(8,128)}, bf16[4,512,1536]{2,1,0:T(8,128)(2,1)}) fusion(f32[4,512,3072]{2,1,0:T(8,128)} %fusion.34, bf16[4,512,576]{1,2,0:T(8,128)(2,1)S(1)} %copy-done.43, bf16[1536,576]{1,0:T(8,128)(2,1)S(1)} %copy-done.45), kind=kOutput, calls=%fused_computation.50 | convolution fusion | flops 3667918848 | bytes 60751872 | tf_op jit(solution)/shard_map/iou,eu->ioe/dot_general | solution.py:413
  237.6 16.0 %bitcast_convert_fusion = bf16[576,3072]{1,0:T(8,128)(2,1)} fusion(f32[4,512,1536]{2,1,0:T(8,128)} %get-tuple-element.48, f32[4,512,1536]{2,1,0:T(8,128)} %get-tuple-element.47, f32[4,512,576]{1,2,0:T(8,128)} %get-tuple-element.83, f32[576]{0:T(1024)S(1)} %copy-done.55, f32[4,512]{1,0:T(4,128)S(1)} %fusion.27), kind=kOutput, calls=%fused_computation.12 | convolution fusion | flops 7265648640 | bytes 33433856 | tf_op jit(solution)/shard_map/bqg,bqv->gv/dot_general | solution.py:417
  253.6 16.1 %multiply_reduce_fusion = (bf16[576]{0:T(1024)(128)(2,1)S(1)}, f32[4,512]{1,0:T(4,128)S(1)}, f32[4,512,576]{1,2,0:T(8,128)}) fusion(f32[4,512,576]{1,2,0:T(8,128)} %get-tuple-element.83, f32[4,512]{1,0:T(4,128)S(1)} %fusion.27, f32[576]{0:T(1024)S(1)} %copy-done.55, bf16[576,3072,1]{1,0,2:T(8,128)(2,1)} %reshape.184, ...), kind=kOutput, calls=%fused_computation.24 | convolution fusion | flops 7267415552 | bytes 38161792 | tf_op jit(solution)/shard_map/evi,ai->eva/dot_general | solution.py:420
  269.7 7.4 %reshape.170 = bf16[16,2,55296]{2,1,0:T(2,128)(2,1)} reshape(bf16[576,3072]{1,0:T(8,128)(2,1)} %bitcast_convert_fusion) | data formatting | bytes 7077888 | tf_op jit(solution)/shard_map/reshape | solution.py:433
  277.0 5.0 copy.110
  282.0 6.2 %fusion.3 = f32[4,512,576]{1,2,0:T(8,128)} fusion(bf16[4,512,576]{1,2,0:T(8,128)(2,1)S(1)} %copy-done.44, f32[4,512,576]{1,2,0:T(8,128)} %get-tuple-element.83, f32[4,512,576]{1,2,0:T(8,128)S(1)} %copy-done.42, f32[4,512]{1,0:T(4,128)S(1)} %multiply_multiply_fusion.1, f32[576]{0:T(1024)S(1)} %copy-done.55, f32[4,512]{1,0:T(4,128)S(1)} %fusion.27), kind=kLoop, calls=%fused_computation.17 | loop fusion | flops 8257536 | bytes 16533760 | tf_op jit(solution)/shard_map/add | solution.py:425
  294.7 8.6 %bitcast_convert_fusion.1 = bf16[1536,576]{0,1:T(8,128)(2,1)} fusion(bf16[4,512,576]{1,2,0:T(8,128)(2,1)} %param.15, bf16[4,512,1536]{2,1,0:T(8,128)(2,1)} %get-tuple-element.49), kind=kOutput, calls=%fused_computation.30 | convolution fusion | flops 3624763392 | bytes 10420224 | tf_op jit(solution)/shard_map/rqh,rqo->ho/dot_general | solution.py:410
  307.1 5.6 %reshape.171 = bf16[16,2,27648]{2,1,0:T(2,128)(2,1)} reshape(bf16[1536,576]{1,0:T(8,128)(2,1)} %copy.108) | data formatting | bytes 3538944 | tf_op jit(solution)/shard_map/reshape | solution.py:433
  315.7 4.9 convolution_convert_fusion
  321.9 9.4 %shard_map.137 = (bf16[1,512,576]{2,1,0:T(8,128)(2,1)S(1)}, bf16[1,512,384]{2,1,0:T(8,128)(2,1)S(1)}, f32[1,512,384]{2,1,0:T(8,128)S(1)}) custom-call(s32[1,4]{1,0:T(1,128)S(1)} %copy-done.25, bf16[1,576,512]{2,1,0:T(8,128)(2,1)S(1)} %copy-done.2, bf16[1,512,576]{2,1,0:T(8,128)(2,1)S(1)} %get-tuple-element.50.delta_ref, ...), custom_call_target="tpu_custom_call" | custom-call | flops 6039797760 | bytes 4194304 | tf_op jit(solution)/shard_map/pallas_call | solution.py:338
  332.3 10.6 %shard_map.138 = (bf16[1,512,576]{2,1,0:T(8,128)(2,1)S(1)}, bf16[1,512,384]{2,1,0:T(8,128)(2,1)S(1)}, f32[1,512,384]{2,1,0:T(8,128)S(1)}) custom-call(s32[1,4]{1,0:T(1,128)S(1)} %copy-done.24, bf16[1,576,512]{2,1,0:T(8,128)(2,1)S(1)} %get-tuple-element.57.queries_ref, bf16[1,512,576]{2,1,0:T(8,128)(2,1)S(1)} %get-tuple-element.53.delta_ref, ...), custom_call_target="tpu_custom_call" | custom-call | flops 6039797760 | bytes 4194304 | tf_op jit(solution)/shard_map/pallas_call | solution.py:338
  343.7 10.8 %shard_map.139 = (bf16[1,512,576]{2,1,0:T(8,128)(2,1)S(1)}, bf16[1,512,384]{2,1,0:T(8,128)(2,1)S(1)}, f32[1,512,384]{2,1,0:T(8,128)S(1)}) custom-call(s32[1,4]{1,0:T(1,128)S(1)} %copy-done.23, bf16[1,576,512]{2,1,0:T(8,128)(2,1)S(1)} %get-tuple-element.56.queries_ref, bf16[1,512,576]{2,1,0:T(8,128)(2,1)S(1)} %get-tuple-element.52.delta_ref, ...), custom_call_target="tpu_custom_call" | custom-call | flops 6039797760 | bytes 4194304 | tf_op jit(solution)/shard_map/pallas_call | solution.py:338
  355.4 10.8 %shard_map.140 = (bf16[1,512,576]{2,1,0:T(8,128)(2,1)S(1)}, bf16[1,512,384]{2,1,0:T(8,128)(2,1)S(1)}, f32[1,512,384]{2,1,0:T(8,128)S(1)}) custom-call(s32[1,4]{1,0:T(1,128)S(1)} %copy-done.22, bf16[1,576,512]{2,1,0:T(8,128)(2,1)S(1)} %copy-done.1, bf16[1,512,576]{2,1,0:T(8,128)(2,1)S(1)} %get-tuple-element.51.delta_ref, f32[1,4,8,384]{3,2,1,0:T(8,128)S(1)} %copy-done.13, ...), custom_call_target="tpu_custom_call" | custom-call | flops 6039797760 | bytes 4194304 | tf_op jit(solution)/shard_map/pallas_call | solution.py:338
  368.9 5.7 %pad_maximum_fusion = bf16[16,2,93312]{2,0,1:T(8,128)(2,1)} fusion(bf16[16,2,10368]{2,0,1:T(8,128)(2,1)} %copy.112, bf16[16,2,27648]{2,0,1:T(8,128)(2,1)} %copy.111, bf16[16,2,55296]{2,0,1:T(8,128)(2,1)} %copy.110), kind=kLoop, calls=%fused_computation.16 | loop fusion | flops 17915904 | bytes 11943936 | tf_op jit(solution)/shard_map/concatenate | solution.py:51
  374.6 7.1 %reshape.173 = bf16[16,2,729,128]{3,2,0,1:T(8,128)(2,1)} reshape(bf16[16,2,93312]{2,0,1:T(8,128)(2,1)} %pad_maximum_fusion) | data formatting | bytes 11943936 | tf_op jit(solution)/shard_map/reshape | solution.py:53
  386.6 13.8 %collective-permute-start.7 = (bf16[16,729,128]{2,0,1:T(8,128)(2,1)}, bf16[16,729,128]{2,0,1:T(8,128)(2,1)}, u32[]{:S(2)}, u32[]{:S(2)}) collective-permute-start(bf16[16,729,128]{2,0,1:T(8,128)(2,1)} %bitcast.94), channel_id=1, source_target_pairs={{0,1},{1,0},{2,3},{3,2},{4,5},{5,4},{6,7},{7,6},{8,9},{9,8},{10,11... | collective-permute-start | bytes 8957960 | tf_op jit(solution)/shard_map/ppermute | solution.py:43
  403.7 5.3 %bitcast_convert_fusion.2 = bf16[576,960]{1,0:T(8,128)(2,1)} fusion(bf16[4,512,576]{2,1,0:T(8,128)(2,1)S(1)} %copy-done.57, bf16[4,512,384]{2,1,0:T(8,128)(2,1)S(1)} %fusion.10, bf16[1,512,576]{2,1,0:T(8,128)(2,1)S(1)} %copy-done.36, bf16[1,512,576]{2,1,0:T(8,128)(2,1)S(1)} %copy-done.33, bf16[1,512,576]{2,1,0:T(8,128)(2,1)S(1)} %copy-done.30, ...), kind=kOutput, calls=%fused_computation.36 | convolution fusion | flops 2285137920 | bytes 7397376 | tf_op jit(solution)/shard_map/zgv,zgf->vf/dot_general | solution.py:451
  412.4 7.0 %fusion.9 = (bf16[576]{0:T(1024)(128)(2,1)S(1)}, f32[4,512]{1,0:T(4,128)S(1)}, f32[4,512,576]{1,2,0:T(8,128)}) fusion(bf16[4,512,576]{1,2,0:T(8,128)(2,1)} %param.8, f32[4,512]{1,0:T(4,128)S(1)} %copy-done.52, f32[576]{0:T(1024)S(1)} %copy-done.54, bf16[576,960,1]{1,0,2:T(8,128)(2,1)} %reshape.188, bf16[4,512,384]{2,1,0:T(8,128)(2,1)} %copy-done.47, ...), kind=kOutput, calls=%fused_computation.23 | convolution fusion | flops 2292839936 | bytes 12135808 | tf_op jit(solution)/shard_map/xgc,fc->xgf/dot_general | solution.py:454
  431.6 8.1 %add_convert_fusion.1 = bf16[4,512,576]{1,2,0:T(8,128)(2,1)} fusion(f32[4,512,576]{1,2,0:T(8,128)S(1)} %bitcast.104, bf16[4,512,1536]{2,1,0:T(8,128)(2,1)} %get-tuple-element.49, bf16[1536,576]{1,0:T(8,128)(2,1)S(1)} %copy-done.46), kind=kOutput, calls=%fused_computation.26 | convolution fusion | flops 3626237952 | bytes 15138816 | tf_op jit(solution)/shard_map/gvc,cr->gvr/dot_general | solution.py:408
  439.7 30.5 %collective-permute-done.3 = bf16[8,136,128]{2,1,0:T(8,128)(2,1)S(1)} collective-permute-done((bf16[8,136,128]{2,1,0:T(8,128)(2,1)S(1)}, bf16[8,136,128]{2,1,0:T(8,128)(2,1)S(1)}, u32[]{:S(2)}, u32[]{:S(2)}) %collective-permute-start.3) | collective-permute-done | bytes 278560 | tf_op jit(solution)/shard_map/ppermute | solution.py:43
  486.7 5.5 %collective-permute-done.9 = bf16[4,729,128]{2,0,1:T(4,128)(2,1)S(1)} collective-permute-done((bf16[4,729,128]{2,0,1:T(4,128)(2,1)S(1)}, bf16[4,729,128]{2,0,1:T(4,128)(2,1)S(1)}, u32[]{:S(2)}, u32[]{:S(2)}) %collective-permute-start.9) | collective-permute-done | bytes 746528 | tf_op jit(solution)/shard_map/ppermute | solution.py:43
  494.7 5.5 %fusion.5 = bf16[4,512,576]{1,2,0:T(8,128)(2,1)} fusion(f32[4,512,576]{1,2,0:T(8,128)} %fusion.3, bf16[4,512,576]{1,2,0:T(8,128)(2,1)S(1)} %copy-done.39, f32[4,512,576]{1,2,0:T(8,128)S(1)} %bitcast.102, f32[4,512]{1,0:T(4,128)S(1)} %multiply_multiply_fusion, f32[4,512]{1,0:T(4,128)S(1)} %copy-done.52, f32[576]{0:T(1024)S(1)} %copy-done.54), kind=kLoop, calls=%fused_computation.19 | loop fusion | flops 9437184 | bytes 14174464 | tf_op jit(solution)/shard_map/convert_element_type | solution.py:459
  507.4 5.5 %collective-permute-done.11 = bf16[1,729,128]{2,1,0:T(8,128)(2,1)S(1)} collective-permute-done((bf16[1,729,128]{2,1,0:T(8,128)(2,1)S(1)}, bf16[1,729,128]{2,1,0:T(8,128)(2,1)S(1)}, u32[]{:S(2)}, u32[]{:S(2)}) %collective-permute-start.11) | collective-permute-done | bytes 186656 | tf_op jit(solution)/shard_map/ppermute | solution.py:43
  (234 shorter events, 116.7 us)
Async XLA Ops:
  7.2 62.5 %all-gather.5.cloned.1.call-start = ((), (), s32[]{:S(2)}) async-start(), calls=%async_computation | async-start | bytes 1148928 | tf_op jit(solution)/shard_map/all_gather | solution.py:369
  9.4 118.1 %all-gather.9.cloned.1.call-start = ((), (), s32[]{:S(2)}) async-start(), calls=%async_computation.2 | async-start | bytes 1824768 | tf_op jit(solution)/shard_map/all_gather | solution.py:375
  10.1 179.4 %all-gather.7.cloned.1.call-start = ((), (), s32[]{:S(2)}) async-start(), calls=%async_computation.1 | async-start | bytes 3649536 | tf_op jit(solution)/shard_map/all_gather | solution.py:374
  82.5 19.5 %copy-start.41 = (bf16[32,17280]{1,0:T(8,128)(2,1)S(1)}, bf16[32,17280]{1,0:T(8,128)(2,1)}, u32[]{:S(2)}) copy-start(bf16[32,17280]{1,0:T(8,128)(2,1)} %copy-done.40) | copy-start | bytes 3317764
  82.5 49.3 %collective-permute-start = (bf16[4,512,384]{2,1,0:T(8,128)(2,1)}, bf16[4,512,384]{2,1,0:T(8,128)(2,1)}, u32[]{:S(2)}, u32[]{:S(2)}) collective-permute-start(bf16[4,512,384]{2,1,0:T(8,128)(2,1)} %get-tuple-element.25.near_ref), channel_id=1, source_target_pairs={{0,1},{2,3},{4,5},{6,7},{8,9},{10,11},{12,13},{14,15},{16,17},{18,... | collective-permute-start | bytes 4718600 | tf_op jit(solution)/shard_map/ppermute | solution.py:34
  86.2 17.7 %copy-start.16 = (s32[4,4]{1,0:T(4,128)}, s32[4,4]{1,0:T(4,128)S(1)}, u32[]{:S(2)}) copy-start(s32[4,4]{1,0:T(4,128)S(1)} %add_select_fusion.first_ref) | copy-start | bytes 196
  132.5 26.2 %copy-start.38 = (bf16[4,512,576]{1,2,0:T(8,128)(2,1)S(1)}, bf16[4,512,576]{1,2,0:T(8,128)(2,1)}, u32[]{:S(2)}) copy-start(bf16[4,512,576]{1,2,0:T(8,128)(2,1)} %param.8) | copy-start | bytes 7077892
  132.5 26.2 %copy-start.49 = (bf16[576,576]{1,0:T(8,128)(2,1)S(1)}, bf16[576,576]{1,0:T(8,128)(2,1)}, u32[]{:S(2)}) copy-start(bf16[576,576]{1,0:T(8,128)(2,1)} %reshape.162) | copy-start | bytes 1990660
  168.0 28.1 %copy-start.55 = (f32[576]{0:T(1024)S(1)}, f32[576]{0:T(1024)}, u32[]{:S(2)}) copy-start(f32[576]{0:T(1024)} %slice.165) | copy-start | bytes 6916
  196.1 17.8 %copy-start.43 = (bf16[4,512,576]{1,2,0:T(8,128)(2,1)S(1)}, bf16[4,512,576]{1,2,0:T(8,128)(2,1)}, u32[]{:S(2)}) copy-start(bf16[4,512,576]{1,2,0:T(8,128)(2,1)} %param.15) | copy-start | bytes 7077892
  196.1 17.8 %copy-start.45 = (bf16[1536,576]{1,0:T(8,128)(2,1)S(1)}, bf16[1536,576]{1,0:T(8,128)(2,1)}, u32[]{:S(2)}) copy-start(bf16[1536,576]{1,0:T(8,128)(2,1)} %reshape.164) | copy-start | bytes 5308420
  332.2 11.4 %copy-start.4 = (bf16[1,512,384]{2,1,0:T(8,128)(2,1)S(1)}, bf16[1,512,384]{2,1,0:T(8,128)(2,1)}, u32[]{:S(2)}) copy-start(bf16[1,512,384]{2,1,0:T(8,128)(2,1)} %get-tuple-element.60.near_ref) | copy-start | bytes 1179652
  343.7 11.7 %copy-start.1 = (bf16[1,576,512]{2,1,0:T(8,128)(2,1)S(1)}, bf16[1,576,512]{2,1,0:T(8,128)(2,1)}, u32[]{:S(2)}) copy-start(bf16[1,576,512]{2,1,0:T(8,128)(2,1)} %get-tuple-element.55.queries_ref) | copy-start | bytes 1769476
  343.7 11.7 %copy-start.3 = (bf16[1,512,384]{2,1,0:T(8,128)(2,1)S(1)}, bf16[1,512,384]{2,1,0:T(8,128)(2,1)}, u32[]{:S(2)}) copy-start(bf16[1,512,384]{2,1,0:T(8,128)(2,1)} %get-tuple-element.59.near_ref) | copy-start | bytes 1179652
  343.7 11.7 %copy-start.6 = (bf16[1,512,384]{2,1,0:T(8,128)(2,1)S(1)}, bf16[1,512,384]{2,1,0:T(8,128)(2,1)}, u32[]{:S(2)}) copy-start(bf16[1,512,384]{2,1,0:T(8,128)(2,1)} %get-tuple-element.63.far_ref) | copy-start | bytes 1179652
  343.7 11.7 %copy-start.13 = (f32[1,4,8,384]{3,2,1,0:T(8,128)S(1)}, f32[1,4,8,384]{3,2,1,0:T(8,128)}, u32[]{:S(2)}) copy-start(f32[1,4,8,384]{3,2,1,0:T(8,128)} %get-tuple-element.67.log_ref) | copy-start | bytes 147460
  343.7 11.7 %copy-start.18 = (f32[1,1,1024]{2,1,0:T(1,128)S(1)}, f32[1,1,1024]{2,1,0:T(1,128)}, u32[]{:S(2)}) copy-start(f32[1,1,1024]{2,1,0:T(1,128)} %get-tuple-element.71.labels_ref) | copy-start | bytes 12292
  343.7 11.7 %copy-start.22 = (s32[1,4]{1,0:T(1,128)S(1)}, s32[1,4]{1,0:T(1,128)}, u32[]{:S(2)}) copy-start(s32[1,4]{1,0:T(1,128)} %get-tuple-element.79.first_ref) | copy-start | bytes 52
  367.6 32.8 %collective-permute-start.1 = (bf16[4,512,384]{2,1,0:T(8,128)(2,1)}, bf16[4,512,384]{2,1,0:T(8,128)(2,1)}, u32[]{:S(2)}, u32[]{:S(2)}) collective-permute-start(bf16[4,512,384]{2,1,0:T(8,128)(2,1)} %pad_maximum_fusion.2), channel_id=1, source_target_pairs={{1,0},{3,2},{5,4},{7,6},{9,8},{11,10},{13,12},{15,14},{17,16},{19,... | collective-permute-start | bytes 4718600 | tf_op jit(solution)/shard_map/ppermute | solution.py:34
  386.6 38.3 %collective-permute-start.7 = (bf16[16,729,128]{2,0,1:T(8,128)(2,1)}, bf16[16,729,128]{2,0,1:T(8,128)(2,1)}, u32[]{:S(2)}, u32[]{:S(2)}) collective-permute-start(bf16[16,729,128]{2,0,1:T(8,128)(2,1)} %bitcast.94), channel_id=1, source_target_pairs={{0,1},{1,0},{2,3},{3,2},{4,5},{5,4},{6,7},{7,6},{8,9},{9,8},{10,11... | collective-permute-start | bytes 8957960 | tf_op jit(solution)/shard_map/ppermute | solution.py:43
  422.7 2.0 collective-permute-start.2
  429.4 43.3 %collective-permute-start.8 = (bf16[8,729,128]{2,0,1:T(8,128)(2,1)S(1)}, bf16[8,729,128]{2,0,1:T(8,128)(2,1)S(1)}, u32[]{:S(2)}, u32[]{:S(2)}) collective-permute-start(bf16[8,729,128]{2,0,1:T(8,128)(2,1)S(1)} %bitcast.111), channel_id=1, source_target_pairs={{0,2},{2,0},{4,6},{6,4},{8,10},{10,8},{12,14},{14,12},{16,18},{18,... | collective-permute-start | bytes 4478984 | tf_op jit(solution)/shard_map/ppermute | solution.py:43
  431.3 38.9 %collective-permute-start.3 = (bf16[8,136,128]{2,1,0:T(8,128)(2,1)S(1)}, bf16[8,136,128]{2,1,0:T(8,128)(2,1)S(1)}, u32[]{:S(2)}, u32[]{:S(2)}) collective-permute-start(bf16[8,136,128]{2,1,0:T(8,128)(2,1)S(1)} %fusion.24), channel_id=1, source_target_pairs={{0,2},{2,0},{4,6},{6,4},{8,10},{10,8},{12,14},{14,12},{16,18},{18,... | collective-permute-start | bytes 835592 | tf_op jit(solution)/shard_map/ppermute | solution.py:43
  470.2 24.5 %slice-start = ((s8[4718592]{0:T(1024)(128)(4,1)}), s8[4194304]{0:T(1024)(128)(4,1)S(1)}, s32[]{:S(2)}) async-start(s8[4718592]{0:T(1024)(128)(4,1)} %bitcast.101), calls=%async_computation.3 | async-start | bytes 8388608
  470.3 24.4 %slice-start.1 = ((s8[4718592]{0:T(1024)(128)(4,1)}), s8[524288]{0:T(1024)(128)(4,1)S(1)}, s32[]{:S(2)}) async-start(s8[4718592]{0:T(1024)(128)(4,1)} %bitcast.101), calls=%async_computation.4 | async-start | bytes 1048576
  470.3 6.5 %collective-permute-start.4 = (bf16[4,136,128]{2,1,0:T(8,128)(2,1)S(1)}, bf16[4,136,128]{2,1,0:T(8,128)(2,1)S(1)}, u32[]{:S(2)}, u32[]{:S(2)}) collective-permute-start(bf16[4,136,128]{2,1,0:T(8,128)(2,1)S(1)} %fusion.25), channel_id=1, source_target_pairs={{0,4},{2,6},{4,0},{6,2},{8,12},{10,14},{12,8},{14,10},{16,20},{18,... | collective-permute-start | bytes 417800 | tf_op jit(solution)/shard_map/ppermute | solution.py:43
  473.0 21.7 %copy-start.39 = (bf16[4,512,576]{1,2,0:T(8,128)(2,1)S(1)}, bf16[4,512,576]{1,2,0:T(8,128)(2,1)}, u32[]{:S(2)}) copy-start(bf16[4,512,576]{1,2,0:T(8,128)(2,1)} %param.8) | copy-start | bytes 7077892
  473.5 18.7 %collective-permute-start.9 = (bf16[4,729,128]{2,0,1:T(4,128)(2,1)S(1)}, bf16[4,729,128]{2,0,1:T(4,128)(2,1)S(1)}, u32[]{:S(2)}, u32[]{:S(2)}) collective-permute-start(bf16[4,729,128]{2,0,1:T(4,128)(2,1)S(1)} %copy.117), channel_id=1, source_target_pairs={{0,4},{2,6},{4,0},{6,2},{8,12},{10,14},{12,8},{14,10},{16,20},{18,... | collective-permute-start | bytes 2239496 | tf_op jit(solution)/shard_map/ppermute | solution.py:43
  476.9 5.0 collective-permute-start.5
  481.9 18.2 %collective-permute-start.6 = (bf16[1,136,128]{2,1,0:T(8,128)(2,1)S(1)}, bf16[1,136,128]{2,1,0:T(8,128)(2,1)S(1)}, u32[]{:S(2)}, u32[]{:S(2)}) collective-permute-start(bf16[1,136,128]{2,1,0:T(8,128)(2,1)S(1)} %dynamic-slice_convert_fusion.7), channel_id=1, source_target_pairs={{0,16},{2,18},{4,20},{6,22},{8,24},{10,26},{12,28},{14,30},{16,0},... | collective-permute-start | bytes 104456 | tf_op jit(solution)/shard_map/ppermute | solution.py:43
  492.4 10.2 %collective-permute-start.10 = (bf16[2,729,128]{2,1,0:T(8,128)(2,1)S(1)}, bf16[2,729,128]{2,1,0:T(8,128)(2,1)S(1)}, u32[]{:S(2)}, u32[]{:S(2)}) collective-permute-start(bf16[2,729,128]{2,1,0:T(8,128)(2,1)S(1)} %fusion.23), channel_id=1, source_target_pairs={{0,8},{2,10},{4,12},{6,14},{8,0},{10,2},{12,4},{14,6},{16,24},{18,... | collective-permute-start | bytes 1119752 | tf_op jit(solution)/shard_map/ppermute | solution.py:43
  502.7 10.2 %collective-permute-start.11 = (bf16[1,729,128]{2,1,0:T(8,128)(2,1)S(1)}, bf16[1,729,128]{2,1,0:T(8,128)(2,1)S(1)}, u32[]{:S(2)}, u32[]{:S(2)}) collective-permute-start(bf16[1,729,128]{2,1,0:T(8,128)(2,1)S(1)} %dynamic-slice_convert_fusion.4), channel_id=1, source_target_pairs={{0,16},{2,18},{4,20},{6,22},{8,24},{10,26},{12,28},{14,30},{16,0},... | collective-permute-start | bytes 559880 | tf_op jit(solution)/shard_map/ppermute | solution.py:43
  (45 other events, 243.9 us)
Sparse Core Ops, SparseCore 0:
  11.5 58.1 all-gather.4
  72.5 54.9 all-gather.8
  130.4 59.0 all-gather.6

commit v2 on v1

--- a/solution.py
+++ b/solution.py
@@ -34,34 +34,56 @@
     return lax.ppermute(block, axis, route)
 
 
-def halved(block, axis, bit):
-    size = lax.axis_size(axis)
+def away_and_kept(block, axis, bit, place):
     mine = (lax.axis_index(axis) // bit) % 2
-    low = block.astype(jnp.bfloat16)
-    away = lax.dynamic_index_in_dim(low, 1 - mine, axis=1, keepdims=False)
-    kept = lax.dynamic_index_in_dim(block, mine, axis=1, keepdims=False)
-    came = lax.ppermute(away, axis, [(i, i ^ bit) for i in range(size)])
-    return kept.astype(jnp.float32) + came.astype(jnp.float32)
-
-
-def reduce_scatter(parts, shards, halves):
-    sizes = [part.shape[-1] for part in parts]
-    total = sum(sizes)
-    padded = -(-total // 128) * 128
+    parted = block.reshape((-1, 2, place) + block.shape[1:])
+    tail = block.shape[1:]
+    away = lax.dynamic_index_in_dim(parted, 1 - mine, axis=1, keepdims=False).reshape((-1,) + tail)
+    kept = lax.dynamic_index_in_dim(parted, mine, axis=1, keepdims=False).reshape((-1,) + tail)
+    return away.astype(jnp.bfloat16), kept
+
+
+def exchanged(away, axis, bit):
+    return lax.ppermute(away, axis, [(i, i ^ bit) for i in range(lax.axis_size(axis))])
+
+
+def steps_of(shards, swapped):
+    bits = []
+    while 2 ** len(bits) < shards:
+        bits.append(2 ** len(bits))
+    steps = [("seq", 1, 1)]
+    if swapped and len(bits) > 1:
+        steps += [("fsdp", 2, 2), ("fsdp", 1, 1)]
+        bits = bits[2:]
+    return steps + [("fsdp", bit, 1) for bit in bits]
+
+
+def joined_parts(parts):
+    total = sum(part.shape[-1] for part in parts)
     joined = jnp.concatenate([part.astype(jnp.bfloat16) for part in parts], axis=-1)
-    joined = jnp.pad(joined, ((0, 0), (0, 0), (0, padded - total)))
-    block = joined.reshape(shards, halves, padded // 128, 128)
-    block = halved(block, "seq", 1)
-    bit = 1
-    while bit < shards:
-        block = halved(block.reshape(-1, 2, padded // 128, 128), "fsdp", bit)
-        bit *= 2
+    joined = jnp.pad(joined, ((0, 0), (0, 0), (0, -total % 128)))
+    return joined.reshape(joined.shape[0] * joined.shape[1], -1, 128)
+
+
+def cut_apart(block, parts):
     flat = block.reshape(-1)
     outs, at = [], 0
-    for size in sizes:
-        outs.append(flat[at : at + size])
-        at += size
+    for part in parts:
+        outs.append(flat[at : at + part.shape[-1]])
+        at += part.shape[-1]
     return outs
+
+
+def added(kept, came):
+    return kept.astype(jnp.float32) + came.astype(jnp.float32)
+
+
+def reduce_scatter(parts, shards):
+    block = joined_parts(parts)
+    for axis, bit, place in steps_of(shards, False):
+        away, kept = away_and_kept(block, axis, bit, place)
+        block = added(kept, exchanged(away, axis, bit))
+    return cut_apart(block, parts)
 
 
 def project_kernel(x_ref, gain_ref, weight_ref, cos_ref, sin_ref, normed_ref, queries_ref, kv_ref):
@@ -432,18 +454,37 @@
     def spread(matrix):
         return matrix.astype(jnp.bfloat16).reshape(shards, halves, -1)
 
-    gate_up_gradient, down_gradient, output_gradient = reduce_scatter(
-        [spread(delta_gate_up), spread(delta_down), spread(delta_output)], shards, halves
-    )
-
-    pieces = []
+    wholes = [[spread(delta_gate_up)], [spread(delta_down), spread(delta_output)]]
+    routes = [steps_of(shards, False), steps_of(shards, True)]
+    blocks = [joined_parts(parts) for parts in wholes]
+    pieces, step, pending = [], 0, None
     for i in range(sequences):
+        if pending is None and step < len(routes[0]):
+            pending = [away_and_kept(block, *route[step]) for block, route in zip(blocks, routes)]
+            aways = [away for away, kept in pending]
+            delta_mixed, *aways = lax.optimization_barrier([delta_mixed] + aways)
+            came = [exchanged(away, *route[step][:2]) for away, route in zip(aways, routes)]
         at = slice(i, i + 1)
-        pieces.append(
-            attention_backward(
-                first[at], queries[at], delta_mixed[at], logs[at], far[at], near[at], labels[at], cos, sin
-            )
+        piece = attention_backward(
+            first[at], queries[at], delta_mixed[at], logs[at], far[at], near[at], labels[at], cos, sin
         )
+        if pending is not None and (step != 1 or i >= 2):
+            *piece, came_one, came_two = lax.optimization_barrier(list(piece) + came)
+            blocks = [added(kept, new) for (_, kept), new in zip(pending, (came_one, came_two))]
+            delta_mixed, *blocks = lax.optimization_barrier([delta_mixed] + blocks)
+            pending, step = None, step + 1
+        pieces.append(piece)
+    if pending is not None:
+        blocks = [added(kept, new) for (_, kept), new in zip(pending, came)]
+        step += 1
+    while step < len(routes[0]):
+        for which, route in enumerate(routes):
+            away, kept = away_and_kept(blocks[which], *route[step])
+            blocks[which] = added(kept, exchanged(away, *route[step][:2]))
+        step += 1
+    (gate_up_gradient,) = cut_apart(blocks[0], wholes[0])
+    down_gradient, output_gradient = cut_apart(blocks[1], wholes[1])
+
     delta_queries, delta_far, delta_near = [jnp.concatenate(piece, axis=0) for piece in zip(*pieces)]
     back = shifted(delta_far, "seq", -1)
     delta_kv = (delta_near + back.astype(jnp.float32)).astype(jnp.bfloat16)
@@ -461,7 +502,6 @@
     project_gradient, gains_gradient = reduce_scatter(
         [spread(delta_project), jnp.broadcast_to(delta_gain, (shards, halves, delta_gain.shape[-1]))],
         shards,
-        halves,
     )
     return (
         result,

time: 526 us -> 506 us (0.962); the launches traced: 522 us -> 497 us
  local copies, waits for them, and re-layouts: 93.6 us -> 79.9 us
  waiting for transfers between devices: 95.1 us -> 81.9 us
  other arithmetic: 37.4 us -> 43.1 us
    all_gather x1, waiting for transfers between devices: 1.56 us -> 52.4 us  [per_device(): lax.all_gather(jnp.concatenate([project_weight, gains, fill]), both, axis...]
    ppermute x10 -> x15, waiting for transfers between devices: 51.3 us -> 17.8 us  [exchanged(): lax.ppermute(away, axis, [(i, i ^ bit) for i in range(lax.axis_size(axis))])]
    all_gather x1, waiting for transfers between devices: 19.3 us -> 0.01 us  [per_device(): lax.all_gather(down_weight, both, axis=0, tiled=True).reshape(FF, D)]
    another operation x0 -> x3, local copies, waits for them, and re-layouts: none -> 14.2 us  [away_and_kept(): parted = block.reshape((-1, 2, place) + block.shape[1:])]
    reshape x7 -> x3, local copies, waits for them, and re-layouts: 26.1 us -> 12.6 us  [spread(): return matrix.astype(jnp.bfloat16).reshape(shards, halves, -1)]
    all_gather x1, waiting for transfers between devices: 21.6 us -> 10.3 us  [per_device(): lax.all_gather(gate_up_weight, both, axis=0, tiled=True).reshape(D, 2 * FF)]
    ppermute x10 -> x15, starting transfers between devices: 31.8 us -> 28.8 us  [exchanged(): lax.ppermute(away, axis, [(i, i ^ bit) for i in range(lax.axis_size(axis))])]
    unnamed x126 -> x85, local copies, waits for them, and re-layouts: 11.9 us -> 9.16 us
  transfers between devices with their start and end apart: 15 -> 20, of which waited for: 10 -> 7; matrix products, arithmetic and copies ran while one was open for 19% -> 16% of each run, Pallas kernels for 6% -> 15%
where the time goes in v2:
time: 506 us; the launch traced here: 497 us
  matrix products  122 us (24%)
  waiting for transfers between devices  81.9 us (16%)
  local copies, waits for them, and re-layouts  79.9 us (16%)
  Pallas kernels  73.9 us (15%)
  blocking collectives  47 us (9%)
  other arithmetic  43.1 us (9%)
  starting transfers between devices  33.7 us (7%)
  between operations  14.8 us (3%)
    all_gather x1, waiting for transfers between devices, per_device(): lax.all_gather(jnp.concatenate([project_weight, gains, fill]), both, axis...  52.4 us
    all_gather x1, blocking collectives, per_device(): lax.all_gather(output_weight, both, axis=0, tiled=True).reshape(H * HD, D)  47 us
    pallas_call x4, Pallas kernels, attention_backward(): pl.pallas_call(backward_kernel, grid_spec=grid_spec, out_shape=[jax.Shape...  40.7 us
    ppermute x15, starting transfers between devices, exchanged(): lax.ppermute(away, axis, [(i, i ^ bit) for i in range(lax.axis_size(axis))])  28.8 us
    pallas_call x1, Pallas kernels, attention_forward(): pl.pallas_call(forward_kernel, grid_spec=grid_spec, out_shape=[jax.ShapeD...  25.9 us
    dot_general x1, matrix products, per_device(): jnp.einsum('iou,eu->ioe', cotangent, down_matrix, preferred_element_type=...  23.7 us
    dot_general x1, matrix products, per_device(): jnp.einsum('mar,rw->maw', mixer_input, gate_up_matrix, preferred_element_...  17.8 us
    ppermute x15, waiting for transfers between devices, exchanged(): lax.ppermute(away, axis, [(i, i ^ bit) for i in range(lax.axis_size(axis))])  17.8 us
  transfers between devices with their start and end apart: 20, of which 7 were waited for; matrix products, arithmetic and copies ran while one was open for 16% of the time, Pallas kernels for 15%

profile of v2, /device:TPU:0, one launch (start us, length us, event | category | flops | bytes accessed | tf_op | source)
XLA Modules:
  0.0 496.6 jit_solution(17001657193028777413)
XLA Ops:
  11.5 4.4 copy.125.x_ref
  15.8 52.4 %all-gather.5.cloned.1.call-done = bf16[557056]{0:T(1024)(128)(2,1)} async-done(((bf16[17408]{0:T(1024)(128)(2,1)}), bf16[557056]{0:T(1024)(128)(2,1)}) %all-gather.5.cloned.1.call-update) | async-done | bytes 1114128 | tf_op jit(solution)/shard_map/all_gather | solution.py:391
  73.7 7.3 %shard_map.135 = (bf16[4,512,576]{2,1,0:T(8,128)(2,1)}, bf16[4,576,512]{2,1,0:T(8,128)(2,1)S(1)}, bf16[4,512,384]{2,1,0:T(8,128)(2,1)}) custom-call(bf16[4,512,576]{2,1,0:T(8,128)(2,1)} %copy.125.x_ref, f32[1,576]{1,0:T(1,128)S(1)} %broadcast_in_dim.13.gain_ref, bf16[960,576]{1,0:T(8,128)(2,1)S(1)} %bitcast.122, f32[32,512]{1,0:T(8,128)S(1)} %slice.204.cos_ref, ...), custom_call_target="tpu_custom_call" | custom-call | flops 2264924160 | bytes 8388608 | tf_op jit(solution)/shard_map/pallas_call | solution.py:115
  84.5 47.0 %all-gather = bf16[32,1,10368]{2,1,0:T(2,128)(2,1)} all-gather(bf16[1,1,10368]{2,1,0:T(2,128)(2,1)S(1)} %reshape.302), channel_id=1, replica_groups=mesh['fsdp'=16,'seq'=2] {'fsdp','seq'}, dimensions={0}, use_global_device_ids=true | all-gather | bytes 684288 | tf_op jit(solution)/shard_map/all_gather | solution.py:395
  131.4 5.0 %reduce = bf16[32,10368]{1,0:T(8,128)(2,1)S(1)} reduce(bf16[32,1,10368]{2,1,0:T(2,128)(2,1)} %all-gather, bf16[]{:T(256)} %constant.282), dimensions={1}, to_apply=%all-gather.reduce_sub_computation | reduce | bytes 1327106 | tf_op jit(solution)/shard_map/all_gather | solution.py:395
  143.3 4.7 reshape.272
  148.0 25.9 %shard_map.136 = (bf16[4,512,576]{2,1,0:T(8,128)(2,1)}, f32[4,4,8,384]{3,2,1,0:T(8,128)S(1)}) custom-call(s32[4,4]{1,0:T(4,128)S(1)} %add_select_fusion.first_ref, bf16[4,576,512]{2,1,0:T(8,128)(2,1)S(1)} %get-tuple-element.56.queries_ref, bf16[4,512,384]{2,1,0:T(8,128)(2,1)} %collective-permute-done.far_ref, ...), custom_call_target="tpu_custom_call" | custom-call | flops 9663676416 | bytes 8388608 | tf_op jit(solution)/shard_map/pallas_call | solution.py:249
  173.9 6.1 %multiply_reduce_fusion.2 = (f32[4,512]{1,0:T(4,128)S(1)}, f32[4,512,576]{1,2,0:T(8,128)}) fusion(bf16[4,512,576]{2,1,0:T(8,128)(2,1)} %get-tuple-element.58, bf16[576,576]{1,0:T(8,128)(2,1)S(1)} %copy-done.33, bf16[4,512,576]{1,2,0:T(8,128)(2,1)S(1)} %copy-done.13), kind=kOutput, calls=%fused_computation.26 | convolution fusion | flops 1363671040 | bytes 10108928 | tf_op jit(solution)/shard_map/crz,zm->crm/dot_general | solution.py:419
  180.1 10.3 %all-gather.7.cloned.1.call-done = bf16[1769472]{0:T(1024)(128)(2,1)} async-done(((bf16[55296]{0:T(1024)(128)(2,1)}), bf16[1769472]{0:T(1024)(128)(2,1)}) %all-gather.7.cloned.1.call-update) | async-done | bytes 3538960 | tf_op jit(solution)/shard_map/all_gather | solution.py:396
  190.4 6.6 %reshape.306 = bf16[576,3072,1]{1,0,2:T(8,128)(2,1)} reshape(bf16[1769472]{0:T(1024)(128)(2,1)} %all-gather.7.cloned.1.call-done) | data formatting | bytes 7077888 | tf_op jit(solution)/shard_map/reshape | solution.py:396
  197.0 17.8 %fusion.37 = f32[4,512,3072]{2,1,0:T(8,128)} fusion(bf16[576,3072,1]{1,0,2:T(8,128)(2,1)} %reshape.306, f32[4,512,576]{1,2,0:T(8,128)} %get-tuple-element.145, f32[576]{0:T(1024)S(1)} %slice.159, f32[4,512]{1,0:T(4,128)S(1)} %fusion.30), kind=kOutput, calls=%fused_computation.118 | convolution fusion | flops 7251296256 | bytes 33433856 | tf_op jit(solution)/shard_map/mar,rw->maw/dot_general | solution.py:423
  214.8 23.7 %fusion.17 = (f32[4,512,1536]{2,1,0:T(8,128)}, f32[4,512,1536]{2,1,0:T(8,128)}, bf16[4,512,1536]{2,1,0:T(8,128)(2,1)}) fusion(f32[4,512,3072]{2,1,0:T(8,128)} %fusion.37, bf16[4,512,576]{1,2,0:T(8,128)(2,1)S(1)} %copy-done.25, bf16[1536,576]{1,0:T(8,128)(2,1)S(1)} %copy-done.26), kind=kOutput, calls=%fused_computation.48 | convolution fusion | flops 3667918848 | bytes 60751872 | tf_op jit(solution)/shard_map/iou,eu->ioe/dot_general | solution.py:435
  238.5 16.4 %multiply_reduce_fusion = (bf16[576]{0:T(1024)(128)(2,1)S(1)}, f32[4,512]{1,0:T(4,128)S(1)}, f32[4,512,576]{1,2,0:T(8,128)}) fusion(f32[4,512,576]{1,2,0:T(8,128)} %get-tuple-element.145, f32[4,512]{1,0:T(4,128)S(1)} %fusion.30, f32[576]{0:T(1024)S(1)} %slice.159, bf16[576,3072,1]{1,0,2:T(8,128)(2,1)} %reshape.306, f32[4,512,1536]{2,1,0:T(8,128)} %get-tuple-element.112, ...), kind=kOutput, calls=%fused_computation.22 | convolution fusion | flops 7267415552 | bytes 38161792 | tf_op jit(solution)/shard_map/evi,ai->eva/dot_general | solution.py:442
  254.9 16.0 %bitcast_convert_fusion = bf16[576,3072]{1,0:T(8,128)(2,1)} fusion(f32[4,512,1536]{2,1,0:T(8,128)} %get-tuple-element.112, f32[4,512,1536]{2,1,0:T(8,128)} %get-tuple-element.111, f32[4,512,576]{1,2,0:T(8,128)} %get-tuple-element.145, f32[576]{0:T(1024)S(1)} %slice.159, f32[4,512]{1,0:T(4,128)S(1)} %fusion.30), kind=kOutput, calls=%fused_computation.12 | convolution fusion | flops 7265648640 | bytes 33433856 | tf_op jit(solution)/shard_map/bqg,bqv->gv/dot_general | solution.py:439
  270.9 8.2 %fusion.3 = f32[4,512,576]{1,2,0:T(8,128)} fusion(bf16[4,512,576]{1,2,0:T(8,128)(2,1)} %param.15, f32[4,512,576]{1,2,0:T(8,128)} %get-tuple-element.145, f32[4,512,576]{1,2,0:T(8,128)} %get-tuple-element.146, f32[4,512]{1,0:T(4,128)S(1)} %multiply_multiply_fusion.1, f32[576]{0:T(1024)S(1)} %slice.159, f32[4,512]{1,0:T(4,128)S(1)} %fusion.30), kind=kLoop, calls=%fused_computation.15 | loop fusion | flops 8257536 | bytes 16533760 | tf_op jit(solution)/shard_map/add | solution.py:447
  279.1 5.5 %bitcast_convert_fusion.3 = bf16[576,576]{1,0:T(8,128)(2,1)} fusion(bf16[4,512,576]{2,1,0:T(8,128)(2,1)S(1)} %copy-done.39, f32[4,512,576]{1,2,0:T(8,128)} %fusion.3), kind=kOutput, calls=%fused_computation.47 | convolution fusion | flops 1360465920 | bytes 7741440 | tf_op jit(solution)/shard_map/zxa,zxq->aq/dot_general | solution.py:449
  288.2 8.6 %bitcast_convert_fusion.1 = bf16[1536,576]{0,1:T(8,128)(2,1)} fusion(bf16[4,512,576]{1,2,0:T(8,128)(2,1)} %param.15, bf16[4,512,1536]{2,1,0:T(8,128)(2,1)} %get-tuple-element.113), kind=kOutput, calls=%fused_computation.29 | convolution fusion | flops 3624763392 | bytes 10420224 | tf_op jit(solution)/shard_map/rqh,rqo->ho/dot_general | solution.py:432
  300.7 5.5 %reshape.274 = bf16[16,2,27648]{2,1,0:T(2,128)(2,1)} reshape(bf16[1536,576]{1,0:T(8,128)(2,1)} %copy.131) | data formatting | bytes 3538944 | tf_op jit(solution)/shard_map/reshape | solution.py:455
  306.2 5.4 %pad_maximum_fusion.1 = bf16[16,2,38016]{2,1,0:T(2,128)(2,1)} fusion(bf16[16,2,10368]{2,1,0:T(2,128)(2,1)} %reshape.275, bf16[16,2,27648]{2,1,0:T(2,128)(2,1)} %reshape.274), kind=kLoop, calls=%fused_computation.33 | loop fusion | flops 4866048 | bytes 4866048 | tf_op jit(solution)/shard_map/concatenate | solution.py:63
  311.6 6.8 %reshape.317 = bf16[16,2,1,297,128]{4,3,1,0,2:T(8,128)(2,1)} reshape(bf16[16,2,38016]{2,1,0:T(2,128)(2,1)} %pad_maximum_fusion.1) | data formatting | bytes 4866048 | tf_op jit(solution)/shard_map/reshape;reshape | solution.py:39
  321.1 6.6 %reshape_reshape.9 = bf16[16,2,1,432,128]{4,3,1,0,2:T(8,128)(2,1)} reshape(bf16[576,3072]{1,0:T(8,128)(2,1)} %bitcast_convert_fusion) | data formatting | bytes 7077888 | tf_op jit(solution)/shard_map/reshape;reshape | solution.py:39
  330.6 6.5 %convolution_convert_fusion = bf16[4,512,576]{2,1,0:T(8,128)(2,1)} fusion(bf16[576,576,1]{1,0,2:T(8,128)(2,1)S(1)} %copy-done.32, f32[4,512,576]{1,2,0:T(8,128)} %fusion.3), kind=kOutput, calls=%fused_computation.38 | convolution fusion | flops 1361313792 | bytes 7741440 | tf_op jit(solution)/shard_map/wrc,jc->wrj/dot_general | solution.py:450
  345.1 9.2 %shard_map.137 = (bf16[1,512,576]{2,1,0:T(8,128)(2,1)S(1)}, bf16[1,512,384]{2,1,0:T(8,128)(2,1)S(1)}, f32[1,512,384]{2,1,0:T(8,128)S(1)}) custom-call(s32[1,4]{1,0:T(1,128)S(1)} %get-tuple-element.143.first_ref, bf16[1,576,512]{2,1,0:T(8,128)(2,1)S(1)} %get-tuple-element.119.queries_ref, bf16[1,512,576]{2,1,0:T(8,128)(2,1)S(1)} %slice.164.delta_ref, ...), custom_call_target="tpu_custom_call" | custom-call | flops 6039797760 | bytes 4194304 | tf_op jit(solution)/shard_map/pallas_call | solution.py:360
  363.6 9.4 %shard_map.139 = (bf16[1,512,576]{2,1,0:T(8,128)(2,1)S(1)}, bf16[1,512,384]{2,1,0:T(8,128)(2,1)S(1)}, f32[1,512,384]{2,1,0:T(8,128)S(1)}) custom-call(s32[1,4]{1,0:T(1,128)S(1)} %get-tuple-element.142.first_ref, bf16[1,576,512]{2,1,0:T(8,128)(2,1)S(1)} %get-tuple-element.118.queries_ref, bf16[1,512,576]{2,1,0:T(8,128)(2,1)S(1)} %get-tuple-element.115.delta_ref, ...), custom_call_target="tpu_custom_call" | custom-call | flops 6039797760 | bytes 4194304 | tf_op jit(solution)/shard_map/pallas_call | solution.py:360
  373.1 11.8 %shard_map.138 = (bf16[1,512,576]{2,1,0:T(8,128)(2,1)S(1)}, bf16[1,512,384]{2,1,0:T(8,128)(2,1)S(1)}, f32[1,512,384]{2,1,0:T(8,128)S(1)}) custom-call(s32[1,4]{1,0:T(1,128)S(1)} %get-tuple-element.140.first_ref, bf16[1,576,512]{2,1,0:T(8,128)(2,1)S(1)} %get-tuple-element.116.queries_ref, bf16[1,512,576]{2,1,0:T(8,128)(2,1)S(1)} %get-tuple-element.114.delta_ref, ...), custom_call_target="tpu_custom_call" | custom-call | flops 6039797760 | bytes 4194304 | tf_op jit(solution)/shard_map/pallas_call | solution.py:360
  390.0 10.4 %shard_map.140 = (bf16[1,512,576]{2,1,0:T(8,128)(2,1)S(1)}, bf16[1,512,384]{2,1,0:T(8,128)(2,1)S(1)}, f32[1,512,384]{2,1,0:T(8,128)S(1)}) custom-call(s32[1,4]{1,0:T(1,128)S(1)} %get-tuple-element.141.first_ref, bf16[1,576,512]{2,1,0:T(8,128)(2,1)S(1)} %get-tuple-element.117.queries_ref, bf16[1,512,576]{2,1,0:T(8,128)(2,1)S(1)} %slice.188.delta_ref, ...), custom_call_target="tpu_custom_call" | custom-call | flops 6039797760 | bytes 4194304 | tf_op jit(solution)/shard_map/pallas_call | solution.py:360
  404.9 9.5 %add_convert_fusion.1 = bf16[4,512,576]{1,2,0:T(8,128)(2,1)} fusion(f32[4,512,576]{1,2,0:T(8,128)} %get-tuple-element.145, bf16[4,512,1536]{2,1,0:T(8,128)(2,1)} %get-tuple-element.113, bf16[1536,576]{1,0:T(8,128)(2,1)S(1)} %copy-done.27), kind=kOutput, calls=%fused_computation.24 | convolution fusion | flops 3626237952 | bytes 15138816 | tf_op jit(solution)/shard_map/gvc,cr->gvr/dot_general | solution.py:430
  428.0 5.3 %bitcast_convert_fusion.2 = bf16[576,960]{1,0:T(8,128)(2,1)} fusion(bf16[4,512,576]{2,1,0:T(8,128)(2,1)S(1)} %copy-done.40, bf16[4,512,384]{2,1,0:T(8,128)(2,1)S(1)} %fusion.10, bf16[1,512,576]{2,1,0:T(8,128)(2,1)S(1)} %copy-done.11, bf16[1,512,576]{2,1,0:T(8,128)(2,1)S(1)} %copy-done.5, bf16[1,512,576]{2,1,0:T(8,128)(2,1)S(1)} %copy-done.8, ...), kind=kOutput, calls=%fused_computation.34 | convolution fusion | flops 2285137920 | bytes 7397376 | tf_op jit(solution)/shard_map/zgv,zgf->vf/dot_general | solution.py:492
  436.7 7.1 %fusion.9 = (bf16[576]{0:T(1024)(128)(2,1)S(1)}, f32[4,512]{1,0:T(4,128)S(1)}, f32[4,512,576]{1,2,0:T(8,128)}) fusion(bf16[4,512,576]{1,2,0:T(8,128)(2,1)} %param.8, f32[4,512]{1,0:T(4,128)S(1)} %copy-done.36, f32[576]{0:T(1024)S(1)} %slice.194, bf16[576,960,1]{1,0,2:T(8,128)(2,1)} %reshape.313, bf16[4,512,384]{2,1,0:T(8,128)(2,1)} %copy-done.29, ...), kind=kOutput, calls=%fused_computation.21 | convolution fusion | flops 2292839936 | bytes 12135808 | tf_op jit(solution)/shard_map/xgc,fc->xgf/dot_general | solution.py:495
  446.8 13.6 %collective-permute-start.8 = (bf16[16,136,128]{2,1,0:T(8,128)(2,1)S(1)}, bf16[16,136,128]{2,1,0:T(8,128)(2,1)S(1)}, u32[]{:S(2)}, u32[]{:S(2)}) collective-permute-start(bf16[16,136,128]{2,1,0:T(8,128)(2,1)S(1)} %dynamic-slice_bitcast_fusion.2), channel_id=1, source_target_pairs={{0,1},{1,0},{2,3},{3,2},{4,5},{5,4},{6,7},{7,6},{8,9},{9,8},{10,11... | collective-permute-start | bytes 1671176 | tf_op jit(solution)/shard_map/ppermute | solution.py:47
  465.2 6.6 %collective-permute-done.9 = bf16[8,136,128]{2,1,0:T(8,128)(2,1)S(1)} collective-permute-done((bf16[8,136,128]{2,1,0:T(8,128)(2,1)S(1)}, bf16[8,136,128]{2,1,0:T(8,128)(2,1)S(1)}, u32[]{:S(2)}, u32[]{:S(2)}) %collective-permute-start.9) | collective-permute-done | bytes 278560 | tf_op jit(solution)/shard_map/ppermute | solution.py:47
  483.3 5.4 %fusion.5 = bf16[4,512,576]{1,2,0:T(8,128)(2,1)} fusion(f32[4,512,576]{1,2,0:T(8,128)} %fusion.3, bf16[4,512,576]{1,2,0:T(8,128)(2,1)S(1)} %copy-done.14, f32[4,512,576]{1,2,0:T(8,128)S(1)} %copy-done.21, f32[4,512]{1,0:T(4,128)S(1)} %multiply_multiply_fusion, f32[4,512]{1,0:T(4,128)S(1)} %copy-done.36, f32[576]{0:T(1024)S(1)} %slice.194), kind=kLoop, calls=%fused_computation.17 | loop fusion | flops 9437184 | bytes 14174464 | tf_op jit(solution)/shard_map/convert_element_type | solution.py:500
  (208 shorter events, 97.1 us)
Async XLA Ops:
  7.2 61.0 %all-gather.5.cloned.1.call-start = ((), (), s32[]{:S(2)}) async-start(), calls=%async_computation | async-start | bytes 1148928 | tf_op jit(solution)/shard_map/all_gather | solution.py:391
  9.4 133.9 %all-gather.9.cloned.1.call-start = ((), (), s32[]{:S(2)}) async-start(), calls=%async_computation.2 | async-start | bytes 1824768 | tf_op jit(solution)/shard_map/all_gather | solution.py:397
  10.1 180.3 %all-gather.7.cloned.1.call-start = ((), (), s32[]{:S(2)}) async-start(), calls=%async_computation.1 | async-start | bytes 3649536 | tf_op jit(solution)/shard_map/all_gather | solution.py:396
  81.0 59.0 %copy-start.38 = (s32[4,1024]{1,0:T(4,128)S(1)}, s32[4,1024]{1,0:T(4,128)}, u32[]{:S(2)}) copy-start(s32[4,1024]{1,0:T(4,128)} %param.9) | copy-start | bytes 49156
  81.0 67.0 %collective-permute-start = (bf16[4,512,384]{2,1,0:T(8,128)(2,1)}, bf16[4,512,384]{2,1,0:T(8,128)(2,1)}, u32[]{:S(2)}, u32[]{:S(2)}) collective-permute-start(bf16[4,512,384]{2,1,0:T(8,128)(2,1)} %get-tuple-element.57.near_ref), channel_id=1, source_target_pairs={{0,1},{2,3},{4,5},{6,7},{8,9},{10,11},{12,13},{14,15},{16,17},{18,... | collective-permute-start | bytes 4718600 | tf_op jit(solution)/shard_map/ppermute | solution.py:34
  148.0 25.9 %copy-start.13 = (bf16[4,512,576]{1,2,0:T(8,128)(2,1)S(1)}, bf16[4,512,576]{1,2,0:T(8,128)(2,1)}, u32[]{:S(2)}) copy-start(bf16[4,512,576]{1,2,0:T(8,128)(2,1)} %param.8) | copy-start | bytes 7077892
  148.0 25.9 %copy-start.33 = (bf16[576,576]{1,0:T(8,128)(2,1)S(1)}, bf16[576,576]{1,0:T(8,128)(2,1)}, u32[]{:S(2)}) copy-start(bf16[576,576]{1,0:T(8,128)(2,1)} %reshape.270) | copy-start | bytes 1990660
  197.0 17.8 %copy-start.25 = (bf16[4,512,576]{1,2,0:T(8,128)(2,1)S(1)}, bf16[4,512,576]{1,2,0:T(8,128)(2,1)}, u32[]{:S(2)}) copy-start(bf16[4,512,576]{1,2,0:T(8,128)(2,1)} %param.15) | copy-start | bytes 7077892
  197.0 17.8 %copy-start.26 = (bf16[1536,576]{1,0:T(8,128)(2,1)S(1)}, bf16[1536,576]{1,0:T(8,128)(2,1)}, u32[]{:S(2)}) copy-start(bf16[1536,576]{1,0:T(8,128)(2,1)} %reshape.272) | copy-start | bytes 5308420
  337.1 17.2 %collective-permute-start.1 = (bf16[16,432,128]{2,1,0:T(8,128)(2,1)}, bf16[16,432,128]{2,1,0:T(8,128)(2,1)}, u32[]{:S(2)}, u32[]{:S(2)}) collective-permute-start(bf16[16,432,128]{2,1,0:T(8,128)(2,1)} %dynamic-slice_bitcast_fusion), channel_id=1, source_target_pairs={{0,1},{1,0},{2,3},{3,2},{4,5},{5,4},{6,7},{7,6},{8,9},{9,8},{10,11... | collective-permute-start | bytes 5308424 | tf_op jit(solution)/shard_map/ppermute | solution.py:47
  340.5 13.7 %collective-permute-start.2 = (bf16[16,297,128]{2,0,1:T(8,128)(2,1)}, bf16[16,297,128]{2,0,1:T(8,128)(2,1)S(1)}, u32[]{:S(2)}, u32[]{:S(2)}) collective-permute-start(bf16[16,297,128]{2,0,1:T(8,128)(2,1)} %bitcast.121), channel_id=1, source_target_pairs={{0,1},{1,0},{2,3},{3,2},{4,5},{5,4},{6,7},{7,6},{8,9},{9,8},{10,11... | collective-permute-start | bytes 3649544 | tf_op jit(solution)/shard_map/ppermute | solution.py:47
  361.6 23.4 %collective-permute-start.4 = (bf16[8,297,128]{2,0,1:T(8,128)(2,1)}, bf16[8,297,128]{2,0,1:T(8,128)(2,1)}, u32[]{:S(2)}, u32[]{:S(2)}) collective-permute-start(bf16[8,297,128]{2,0,1:T(8,128)(2,1)} %copy.138), channel_id=1, source_target_pairs={{0,4},{2,6},{4,0},{6,2},{8,12},{10,14},{12,8},{14,10},{16,20},{18,... | collective-permute-start | bytes 1824776 | tf_op jit(solution)/shard_map/ppermute | solution.py:47
  363.0 21.9 %collective-permute-start.3 = (bf16[8,432,128]{2,1,0:T(8,128)(2,1)S(1)}, bf16[8,432,128]{2,1,0:T(8,128)(2,1)S(1)}, u32[]{:S(2)}, u32[]{:S(2)}) collective-permute-start(bf16[8,432,128]{2,1,0:T(8,128)(2,1)S(1)} %fusion.21), channel_id=1, source_target_pairs={{0,2},{2,0},{4,6},{6,4},{8,10},{10,8},{12,14},{14,12},{16,18},{18,... | collective-permute-start | bytes 2654216 | tf_op jit(solution)/shard_map/ppermute | solution.py:47
  373.0 11.9 %copy-start.4 = (bf16[1,512,576]{2,1,0:T(8,128)(2,1)}, bf16[1,512,576]{2,1,0:T(8,128)(2,1)S(1)}, u32[]{:S(2)}) copy-start(bf16[1,512,576]{2,1,0:T(8,128)(2,1)S(1)} %get-tuple-element.79) | copy-start | bytes 1769476
  373.1 13.2 %copy-start.17 = (f32[16,432,128]{2,1,0:T(8,128)S(1)}, f32[16,432,128]{2,1,0:T(8,128)}, u32[]{:S(2)}) copy-start(f32[16,432,128]{2,1,0:T(8,128)} %copy-done.16) | copy-start | bytes 10616836
  387.9 12.5 %collective-permute-start.5 = (bf16[4,432,128]{2,1,0:T(8,128)(2,1)S(1)}, bf16[4,432,128]{2,1,0:T(8,128)(2,1)S(1)}, u32[]{:S(2)}, u32[]{:S(2)}) collective-permute-start(bf16[4,432,128]{2,1,0:T(8,128)(2,1)S(1)} %fusion.23), channel_id=1, source_target_pairs={{0,4},{2,6},{4,0},{6,2},{8,12},{10,14},{12,8},{14,10},{16,20},{18,... | collective-permute-start | bytes 1327112 | tf_op jit(solution)/shard_map/ppermute | solution.py:47
  389.4 11.0 %collective-permute-start.6 = (bf16[4,297,128]{2,1,0:T(8,128)(2,1)S(1)}, bf16[4,297,128]{2,1,0:T(8,128)(2,1)S(1)}, u32[]{:S(2)}, u32[]{:S(2)}) collective-permute-start(bf16[4,297,128]{2,1,0:T(8,128)(2,1)S(1)} %fusion.24), channel_id=1, source_target_pairs={{0,2},{2,0},{4,6},{6,4},{8,10},{10,8},{12,14},{14,12},{16,18},{18,... | collective-permute-start | bytes 912392 | tf_op jit(solution)/shard_map/ppermute | solution.py:47
  400.5 13.9 %copy-start.28 = (f32[4,297,128]{2,1,0:T(8,128)}, f32[4,297,128]{2,1,0:T(8,128)S(1)}, u32[]{:S(2)}) copy-start(f32[4,297,128]{2,1,0:T(8,128)S(1)} %bitcast_add_fusion.3) | copy-start | bytes 1824772
  401.6 15.5 %collective-permute-start.13 = (bf16[2,297,128]{2,1,0:T(8,128)(2,1)S(1)}, bf16[2,297,128]{2,1,0:T(8,128)(2,1)S(1)}, u32[]{:S(2)}, u32[]{:S(2)}) collective-permute-start(bf16[2,297,128]{2,1,0:T(8,128)(2,1)S(1)} %fusion.27), channel_id=1, source_target_pairs={{0,8},{2,10},{4,12},{6,14},{8,0},{10,2},{12,4},{14,6},{16,24},{18,... | collective-permute-start | bytes 456200 | tf_op jit(solution)/shard_map/ppermute | solution.py:47
  403.6 21.3 %collective-permute-start.7 = (bf16[4,512,384]{2,1,0:T(8,128)(2,1)}, bf16[4,512,384]{2,1,0:T(8,128)(2,1)}, u32[]{:S(2)}, u32[]{:S(2)}) collective-permute-start(bf16[4,512,384]{2,1,0:T(8,128)(2,1)} %pad_maximum_fusion.2), channel_id=1, source_target_pairs={{1,0},{3,2},{5,4},{7,6},{9,8},{11,10},{13,12},{15,14},{17,16},{19,... | collective-permute-start | bytes 4718600 | tf_op jit(solution)/shard_map/ppermute | solution.py:34
  415.6 6.0 %collective-permute-start.15 = (bf16[2,432,128]{2,1,0:T(8,128)(2,1)S(1)}, bf16[2,432,128]{2,1,0:T(8,128)(2,1)S(1)}, u32[]{:S(2)}, u32[]{:S(2)}) collective-permute-start(bf16[2,432,128]{2,1,0:T(8,128)(2,1)S(1)} %fusion.26), channel_id=1, source_target_pairs={{0,8},{2,10},{4,12},{6,14},{8,0},{10,2},{12,4},{14,6},{16,24},{18,... | collective-permute-start | bytes 663560 | tf_op jit(solution)/shard_map/ppermute | solution.py:47
  418.2 6.8 %collective-permute-start.14 = (bf16[1,297,128]{2,1,0:T(8,128)(2,1)S(1)}, bf16[1,297,128]{2,1,0:T(8,128)(2,1)S(1)}, u32[]{:S(2)}, u32[]{:S(2)}) collective-permute-start(bf16[1,297,128]{2,1,0:T(8,128)(2,1)S(1)} %dynamic-slice_convert_fusion.8), channel_id=1, source_target_pairs={{0,16},{2,18},{4,20},{6,22},{8,24},{10,26},{12,28},{14,30},{16,0},... | collective-permute-start | bytes 228104 | tf_op jit(solution)/shard_map/ppermute | solution.py:47
  422.8 49.7 %collective-permute-start.16 = (bf16[1,432,128]{2,1,0:T(8,128)(2,1)S(1)}, bf16[1,432,128]{2,1,0:T(8,128)(2,1)S(1)}, u32[]{:S(2)}, u32[]{:S(2)}) collective-permute-start(bf16[1,432,128]{2,1,0:T(8,128)(2,1)S(1)} %dynamic-slice_convert_fusion.7), channel_id=1, source_target_pairs={{0,16},{2,18},{4,20},{6,22},{8,24},{10,26},{12,28},{14,30},{16,0},... | collective-permute-start | bytes 331784 | tf_op jit(solution)/shard_map/ppermute | solution.py:47
  446.0 26.5 %copy-start.31 = (f32[2,432,128]{2,1,0:T(8,128)S(1)}, f32[2,432,128]{2,1,0:T(8,128)}, u32[]{:S(2)}) copy-start(f32[2,432,128]{2,1,0:T(8,128)} %copy-done.30) | copy-start | bytes 1327108
  446.8 30.8 %copy-start.35 = (f32[4,512]{1,0:T(4,128)S(1)}, f32[4,512]{1,0:T(4,128)}, u32[]{:S(2)}) copy-start(f32[4,512]{1,0:T(4,128)} %copy-done.34) | copy-start | bytes 24580
  446.8 36.5 %copy-start.21 = (f32[4,512,576]{1,2,0:T(8,128)S(1)}, f32[4,512,576]{1,2,0:T(8,128)}, u32[]{:S(2)}) copy-start(f32[4,512,576]{1,2,0:T(8,128)} %get-tuple-element.147) | copy-start | bytes 14155780
  446.8 36.5 %copy-start.14 = (bf16[4,512,576]{1,2,0:T(8,128)(2,1)S(1)}, bf16[4,512,576]{1,2,0:T(8,128)(2,1)}, u32[]{:S(2)}) copy-start(bf16[4,512,576]{1,2,0:T(8,128)(2,1)} %param.8) | copy-start | bytes 7077892
  446.8 15.2 %collective-permute-start.8 = (bf16[16,136,128]{2,1,0:T(8,128)(2,1)S(1)}, bf16[16,136,128]{2,1,0:T(8,128)(2,1)S(1)}, u32[]{:S(2)}, u32[]{:S(2)}) collective-permute-start(bf16[16,136,128]{2,1,0:T(8,128)(2,1)S(1)} %dynamic-slice_bitcast_fusion.2), channel_id=1, source_target_pairs={{0,1},{1,0},{2,3},{3,2},{4,5},{5,4},{6,7},{7,6},{8,9},{9,8},{10,11... | collective-permute-start | bytes 1671176 | tf_op jit(solution)/shard_map/ppermute | solution.py:47
  462.2 9.6 %collective-permute-start.9 = (bf16[8,136,128]{2,1,0:T(8,128)(2,1)S(1)}, bf16[8,136,128]{2,1,0:T(8,128)(2,1)S(1)}, u32[]{:S(2)}, u32[]{:S(2)}) collective-permute-start(bf16[8,136,128]{2,1,0:T(8,128)(2,1)S(1)} %fusion.25), channel_id=1, source_target_pairs={{0,2},{2,0},{4,6},{6,4},{8,10},{10,8},{12,14},{14,12},{16,18},{18,... | collective-permute-start | bytes 835592 | tf_op jit(solution)/shard_map/ppermute | solution.py:47
  471.8 5.5 %collective-permute-start.10 = (bf16[4,136,128]{2,1,0:T(8,128)(2,1)S(1)}, bf16[4,136,128]{2,1,0:T(8,128)(2,1)S(1)}, u32[]{:S(2)}, u32[]{:S(2)}) collective-permute-start(bf16[4,136,128]{2,1,0:T(8,128)(2,1)S(1)} %fusion.28), channel_id=1, source_target_pairs={{0,4},{2,6},{4,0},{6,2},{8,12},{10,14},{12,8},{14,10},{16,20},{18,... | collective-permute-start | bytes 417800 | tf_op jit(solution)/shard_map/ppermute | solution.py:47
  477.3 4.4 collective-permute-start.11
  481.8 7.0 %collective-permute-start.12 = (bf16[1,136,128]{2,1,0:T(8,128)(2,1)S(1)}, bf16[1,136,128]{2,1,0:T(8,128)(2,1)S(1)}, u32[]{:S(2)}, u32[]{:S(2)}) collective-permute-start(bf16[1,136,128]{2,1,0:T(8,128)(2,1)S(1)} %dynamic-slice_convert_fusion.10), channel_id=1, source_target_pairs={{0,16},{2,18},{4,20},{6,22},{8,24},{10,26},{12,28},{14,30},{16,0},... | collective-permute-start | bytes 104456 | tf_op jit(solution)/shard_map/ppermute | solution.py:47
  (29 other events, 152.9 us)
Sparse Core Ops, SparseCore 0:
  11.5 56.6 all-gather.4
  71.0 55.8 all-gather.8
  129.8 60.6 all-gather.6
